TPU v7x, 256 devices: a whole 4x4x8 slice. The times are simulated.
256 devices in a mesh: dp: 32 (over x, z), proto: 8 (over y, core).
Axes of the slice: x: 4, y: 4, z: 8, core: 2. Of those that a mesh axis runs over, the one named last changes fastest.
Arguments:
- teacher_feat: bfloat16 [16384, 256], P('dp'), may hold values from -16 to 16
- student_feat: bfloat16 [16384, 256], P('dp'), may hold values from -16 to 16
- teacher_protos: bfloat16 [65536, 256], P('proto'), may hold values from -16 to 16
- student_protos: bfloat16 [65536, 256], P('proto'), may hold values from -16 to 16
Outputs:
- row_loss: float32 [16384], P('dp')
- feature_grad: bfloat16 [16384, 256], P('dp')
- proto_grad: bfloat16 [65536, 256], P(('proto', 'dp'))
All inputs are finite; a program needn't handle non-finite values.
Results may differ from a plain program's by a relative error of at most 0.0069.
Values may be sent and summed in bfloat16 or wider, within the bound.
No kernel may reach another device: no remote copies, remote signals or barrier semaphores. Data moves between devices by JAX's collectives and lax.ppermute only.
A program may use at most 128 MiB of HBM per device.

v0:
```python
import math

import jax
import jax.numpy as jnp
from jax import lax
from jax.experimental import pallas as pl
from jax.experimental.pallas import tpu as pltpu
from jax.sharding import Mesh, PartitionSpec as P

f32 = jnp.float32
bf16 = jnp.bfloat16

NX, NZ, NY, NC = 4, 8, 4, 2
DIM = 256
PROTOS = 65536
BATCH = 16384
ROWS = BATCH // (NX * NZ)
COLS = PROTOS // (NY * NC)
BK = 1024
NB = COLS // BK
T_EXP2 = math.log2(math.e) / 0.07
S_EXP2 = math.log2(math.e) / 0.1
FACTOR = PROTOS / (BATCH * 0.1)
VMEM = 60 * 1024 * 1024
SMALL = 24 * 1024 * 1024
MIDDLE = 48 * 1024 * 1024

NT = (((1,), (1,)), ((), ()))
NN = (((1,), (0,)), ((), ()))


def dot(a, b, dims):
    return lax.dot_general(a, b, dims, preferred_element_type=f32)


def unit_rows(x):
    xf = x.astype(f32)
    return (xf * lax.rsqrt(jnp.sum(xf * xf, axis=1, keepdims=True) + 1e-06)).astype(bf16)


def lane_fold(m):
    acc = m[:, :128]
    for i in range(1, m.shape[1] // 128):
        acc = acc + m[:, i * 128 : (i + 1) * 128]
    return acc


def to_lanes(acc):
    return jnp.sum(acc.T, axis=0, keepdims=True)


def rows4(v):
    return jnp.concatenate([v[:, i * 128 : (i + 1) * 128] for i in range(4)], axis=0)


def lanes512(m):
    return jnp.concatenate([m[i : i + 1] for i in range(4)], axis=1)


def call(kernel, ins, outs, out_shape, scratch, flops, nbytes, name, limit=VMEM):
    return pl.pallas_call(
        kernel,
        in_specs=ins,
        out_specs=outs,
        out_shape=out_shape,
        scratch_shapes=scratch,
        compiler_params=pltpu.CompilerParams(vmem_limit_bytes=limit),
        cost_estimate=pl.CostEstimate(flops=flops, bytes_accessed=nbytes, transcendentals=0),
        name=name,
    )


ANY = pl.BlockSpec(memory_space=pl.ANY)
INSIDE = pl.BlockSpec(memory_space=pltpu.VMEM)
SCALARS = pl.BlockSpec(memory_space=pltpu.SMEM)
DMA = pltpu.SemaphoreType.DMA


def begin(src, dst, sem):
    copy = pltpu.make_async_copy(src, dst, sem)
    copy.start()
    return copy


def begin_blocks(src, dst, sems):
    for j in range(NB):
        begin(src.at[j], dst.at[j], sems.at[j])


def shape(s, t):
    return jax.ShapeDtypeStruct(s, t)


def teacher_kernel(feat, protos, expo_o, cols_o, feat_s, protos_s, expo_s, logit_s, cols_s, sem, in_sems, out_sems):
    first = begin(feat, feat_s, sem)
    begin_blocks(protos, protos_s, in_sems)
    first.wait()
    feat_s[...] = unit_rows(feat_s[...])

    @pl.loop(0, NB)
    def _(j):
        pltpu.make_async_copy(protos.at[j], protos_s.at[j], in_sems.at[j]).wait()
        sums = []
        for n in range(BK // DIM):
            logit_s[n] = dot(feat_s[...], unit_rows(protos_s[j, n * DIM : (n + 1) * DIM, :]), NT)
            acc = jnp.zeros((8, DIM), f32)
            for r in range(0, ROWS, 64):
                e = jnp.exp2(logit_s[n, r : r + 64, :] * T_EXP2)
                expo_s[j, r : r + 64, n * DIM : (n + 1) * DIM] = e.astype(bf16)
                for q in range(0, 64, 8):
                    acc = acc + e[q : q + 8]
            sums.append(jnp.sum(acc, axis=0, keepdims=True))
        cols_s[pl.ds(j, 1), :] = jnp.concatenate(sums, axis=1)
        pltpu.make_async_copy(expo_s.at[j], expo_o.at[j], out_sems.at[j]).start()

    cols_o[...] = jnp.broadcast_to(cols_s[...].astype(bf16)[None], cols_o.shape)
    for j in range(NB):
        pltpu.make_async_copy(expo_s.at[j], expo_o.at[j], out_sems.at[j]).wait()


def teacher(feat, protos):
    return call(
        teacher_kernel,
        [ANY, ANY],
        [ANY, INSIDE],
        [shape((NB, ROWS, BK), bf16), shape((NX * NZ, NB, BK), bf16)],
        [
            pltpu.VMEM((ROWS, DIM), bf16),
            pltpu.VMEM((NB, BK, DIM), bf16),
            pltpu.VMEM((NB, ROWS, BK), bf16),
            pltpu.VMEM((BK // DIM, ROWS, DIM), f32),
            pltpu.VMEM((NB, BK), f32),
            DMA,
            DMA((NB,)),
            DMA((NB,)),
        ],
        2 * ROWS * COLS * DIM,
        ROWS * COLS * 2 + COLS * DIM * 2,
        "teacher",
    )(feat, protos.reshape(NB, BK, DIM))


def student_kernel(
    feat, protos, dirs_o, tot_o, mix_o, feat_s, protos_s, dirs_s, logit_s, exp_s, tot_s, sem, in_sems, out_sems
):
    first = begin(feat, feat_s, sem)
    begin_blocks(protos, protos_s, in_sems)
    first.wait()
    feat_s[...] = unit_rows(feat_s[...])
    tot_s[...] = jnp.zeros_like(tot_s)
    mix_o[...] = jnp.zeros_like(mix_o)

    @pl.loop(0, NB, unroll=2)
    def _(j):
        pltpu.make_async_copy(protos.at[j], protos_s.at[j], in_sems.at[j]).wait()
        for n in range(BK // DIM):
            part = slice(n * DIM, (n + 1) * DIM)
            dirs = unit_rows(protos_s[j, part, :])
            dirs_s[j, part, :] = dirs
            logit_s[n] = dot(feat_s[...], dirs, NT)
            for r in range(0, ROWS, 64):
                e = jnp.exp2(logit_s[n, r : r + 64, :] * S_EXP2)
                exp_s[r : r + 64, part] = e.astype(bf16)
                tot_s[r : r + 64, :] += lane_fold(e)
        mix_o[...] += dot(exp_s[...], dirs_s[j], NN)
        pltpu.make_async_copy(dirs_s.at[j], dirs_o.at[j], out_sems.at[j]).start()

    tot_o[...] = rows4(to_lanes(tot_s[...]))
    for j in range(NB):
        pltpu.make_async_copy(dirs_s.at[j], dirs_o.at[j], out_sems.at[j]).wait()


def student(feat, protos):
    return call(
        student_kernel,
        [ANY, ANY],
        [ANY, INSIDE, INSIDE],
        [shape((NB, BK, DIM), bf16), shape((4, 128), f32), shape((ROWS, DIM), f32)],
        [
            pltpu.VMEM((ROWS, DIM), bf16),
            pltpu.VMEM((NB, BK, DIM), bf16),
            pltpu.VMEM((NB, BK, DIM), bf16),
            pltpu.VMEM((BK // DIM, ROWS, DIM), f32),
            pltpu.VMEM((ROWS, BK), bf16),
            pltpu.VMEM((ROWS, 128), f32),
            DMA,
            DMA((NB,)),
            DMA((NB,)),
        ],
        4 * ROWS * COLS * DIM,
        COLS * DIM * 4,
        "student",
    )(feat, protos.reshape(NB, BK, DIM))


def col_scale(got):
    return 1.0 / (PROTOS * jnp.sum(got[...].astype(f32), axis=0))


def scaled_rows(expo, col, acc_s, j):
    c = col[pl.ds(j, 1), :]
    cs = [c[:, g * 128 : (g + 1) * 128] for g in range(BK // 128)]
    for r in range(0, ROWS, 32):
        acc = acc_s[r : r + 32, :]
        for g in range(BK // 128):
            acc = acc + expo[j, r : r + 32, g * 128 : (g + 1) * 128].astype(f32) * cs[g]
        acc_s[r : r + 32, :] = acc


def row_sums(expo, got, col, acc_s):
    acc_s[...] = jnp.zeros_like(acc_s)
    col[...] = col_scale(got[:, :, :BK])

    @pl.loop(0, NB)
    def _(j):
        scaled_rows(expo, col, acc_s, j)

    return rows4(to_lanes(acc_s[...]))


def row_kernel(expo, got, tot, rows_o, col_s, acc_s, tot_s, sem):
    first = begin(tot, tot_s, sem)
    part = row_sums(expo, got, col_s, acc_s)
    first.wait()
    part = jnp.concatenate([part, tot_s[...]], axis=0)
    rows_o[...] = jnp.broadcast_to(part[None], rows_o.shape)


def row_pass(held, got, tot):
    return call(
        row_kernel,
        [INSIDE, INSIDE, ANY],
        INSIDE,
        shape((NY * NC, 8, 128), f32),
        [pltpu.VMEM((NB, BK), f32), pltpu.VMEM((ROWS, 128), f32), pltpu.VMEM((4, 128), f32), DMA],
        2 * ROWS * COLS,
        1 << 16,
        "row_pass",
        SMALL,
    )(pltpu.with_memory_space_constraint(held, pltpu.VMEM), got, tot)


def row_last_kernel(expo, got, rows_o, col_o, acc_s):
    part = row_sums(expo, got, col_o, acc_s)
    rows_o[...] = jnp.broadcast_to(part[None], rows_o.shape)


def row_last(held, got):
    return call(
        row_last_kernel,
        [INSIDE, INSIDE],
        [INSIDE, INSIDE],
        [shape((NZ * NY * NC, 4, 128), f32), shape((NB, BK), f32)],
        [pltpu.VMEM((ROWS, 128), f32)],
        2 * ROWS * COLS,
        1 << 16,
        "row_last",
        SMALL,
    )(pltpu.with_memory_space_constraint(held, pltpu.VMEM), got)


def col_kernel(expo, got, cols_o, tot_o, scale_s, cols_s):
    total = jnp.sum(got[...], axis=0)
    scale_s[...] = jnp.broadcast_to(1.0 / (BATCH * lanes512(total[:4])), (128, ROWS)).T

    @pl.loop(0, NB)
    def _(j):
        accs = [jnp.zeros((8, 128), f32)] * (BK // 128)
        for r in range(0, ROWS, 32):
            scale = scale_s[r : r + 32, :]
            for g in range(BK // 128):
                t = expo[j, r : r + 32, g * 128 : (g + 1) * 128].astype(f32) * scale
                accs[g] = accs[g] + ((t[0:8] + t[8:16]) + (t[16:24] + t[24:32]))
        cols_s[pl.ds(j, 1), :] = jnp.concatenate(
            [jnp.sum(a, axis=0, keepdims=True) for a in accs], axis=1
        )

    cols_o[...] = jnp.broadcast_to(cols_s[...].astype(bf16)[None], cols_o.shape)
    hi = total[4:].astype(bf16).astype(f32)
    tot_o[...] = jnp.concatenate([hi, total[4:] - hi], axis=0).astype(bf16)


def col_pass(held, got, copies):
    return call(
        col_kernel,
        [INSIDE, INSIDE],
        [INSIDE, INSIDE],
        [shape((copies, NB, BK), bf16), shape((8, 128), bf16)],
        [pltpu.VMEM((ROWS, 128), f32), pltpu.VMEM((NB, BK), f32)],
        2 * ROWS * COLS,
        1 << 20,
        "col_pass",
        SMALL,
    )(pltpu.with_memory_space_constraint(held, pltpu.VMEM), got)


def mix_kernel(expo, col, dirs, feat, mix_o, cross_o, expo_s, dirs_s, feat_s, w_s, sem, sems):
    for j in range(NB):
        begin(expo.at[j], expo_s.at[j], sems.at[0, j])
        begin(dirs.at[j], dirs_s.at[j], sems.at[1, j])
    first = begin(feat, feat_s, sem)
    mix_o[...] = jnp.zeros_like(mix_o)

    @pl.loop(0, NB)
    def _(j):
        pltpu.make_async_copy(expo.at[j], expo_s.at[j], sems.at[0, j]).wait()
        c = col[pl.ds(j, 1), :]
        cs = [c[:, g * 128 : (g + 1) * 128] for g in range(BK // 128)]
        for r in range(0, ROWS, 32):
            for g in range(BK // 128):
                part = slice(g * 128, (g + 1) * 128)
                w_s[r : r + 32, part] = (expo_s[j, r : r + 32, part].astype(f32) * cs[g]).astype(bf16)
        pltpu.make_async_copy(dirs.at[j], dirs_s.at[j], sems.at[1, j]).wait()
        mix_o[...] += dot(w_s[...], dirs_s[j], NN)

    first.wait()
    unit = unit_rows(feat_s[...]).astype(f32)
    cross_o[...] = to_lanes(lane_fold(mix_o[...] * unit)) / 0.1


def mix_pass(expo, col, dirs, feat):
    return call(
        mix_kernel,
        [ANY, INSIDE, ANY, ANY],
        [INSIDE, INSIDE],
        [shape((ROWS, DIM), f32), shape((1, ROWS), f32)],
        [
            pltpu.VMEM((NB, ROWS, BK), bf16),
            pltpu.VMEM((NB, BK, DIM), bf16),
            pltpu.VMEM((ROWS, DIM), bf16),
            pltpu.VMEM((ROWS, BK), bf16),
            DMA,
            DMA((2, NB)),
        ],
        2 * ROWS * COLS * DIM,
        ROWS * COLS * 2 + COLS * DIM * 2,
        "mix_pass",
    )(expo, col, dirs, feat)


def early_kernel(*refs):
    pos, mine, other = refs[0], refs[1 : 1 + NZ], refs[1 + NZ : 1 + 2 * NZ]
    (t_protos, s_dirs, got, rows_o, dirs_o, grad_o,
     raw_s, rows_s, t_s, s_s, got_s, d_s, small, sems, outs) = refs[1 + 2 * NZ :]
    z, core = pos[0], pos[1]
    for k in range(NZ):
        begin(mine[k], raw_s.at[k, core], sems.at[0, k])
        begin(other[k], raw_s.at[k, 1 - core], sems.at[1, k])
        if k == 0:
            first = [begin(t_protos.at[i, z], t_s.at[pl.ds(i * DIM, DIM)], small.at[i]) for i in range(NX)]
            first += [begin(s_dirs.at[i, z], s_s.at[pl.ds(i * DIM, DIM)], small.at[NX + i]) for i in range(NX)]
            first.append(begin(got, got_s, small.at[2 * NX]))
    grad_o[...] = jnp.zeros_like(grad_o)
    for copy in first:
        copy.wait()
    dirs_o[...] = unit_rows(t_s[...])

    @pl.loop(0, NZ)
    def _(k):
        pltpu.make_async_copy(mine[0], raw_s.at[k, core], sems.at[0, k]).wait()
        pltpu.make_async_copy(other[0], raw_s.at[k, 1 - core], sems.at[1, k]).wait()
        total = got_s[pos[3 + k]].astype(f32)[:, BK:]
        scale = FACTOR / lanes512(total[:4] + total[4:])
        half = ROWS // NC
        for h in range(NC):
            part = slice(h * half, (h + 1) * half)
            rows_s[k, part, :DIM] = unit_rows(raw_s[k, h, :, :DIM])
            rows_s[k, part, DIM:] = unit_rows(raw_s[k, h, :, DIM:])
        pltpu.make_async_copy(rows_s.at[k], rows_o.at[k], outs.at[k]).start()
        s_rows = rows_s[k, :, DIM:]
        d_s[...] = (jnp.exp2(dot(s_s[...], s_rows, NT) * S_EXP2) * scale).astype(bf16)
        grad_o[...] += dot(d_s[...], s_rows, NN)

    for k in range(NZ):
        pltpu.make_async_copy(rows_s.at[k], rows_o.at[k], outs.at[k]).wait()


def early(pos, mine, other, t_protos, s_dirs, got):
    n, half = NX * DIM, ROWS // NC
    return call(
        early_kernel,
        [SCALARS] + [ANY] * (2 * NZ + 3),
        [ANY, INSIDE, INSIDE],
        [shape((NZ, ROWS, 2 * DIM), bf16), shape((n, DIM), bf16), shape((n, DIM), f32)],
        [
            pltpu.VMEM((NZ, NC, half, 2 * DIM), bf16),
            pltpu.VMEM((NZ, ROWS, 2 * DIM), bf16),
            pltpu.VMEM((n, DIM), bf16),
            pltpu.VMEM((n, DIM), bf16),
            pltpu.VMEM(got.shape, bf16),
            pltpu.VMEM((n, ROWS), bf16),
            DMA((2 * NX + 1,)),
            DMA((2, NZ)),
            DMA((NZ,)),
        ],
        4 * ROWS * COLS * DIM,
        ROWS * COLS,
        "early",
    )(pos, *mine, *other, t_protos, s_dirs, got)


def down_rows(v):
    return jnp.broadcast_to(v, (128, v.shape[1])).T


def scale_rows(m, scale):
    return jnp.concatenate([m[:, g : g + 128] * scale for g in range(0, m.shape[1], 128)], axis=1)


def grad_kernel(
    pos, dirs, rows, stat, got, student_part, col, s_mix, t_mix, cross,
    own_o, next1_o, next2_o, next3_o, keep_o, give_o, line_o,
    rows_s, got_s, dirs_s, part_s, acc_s, s_mix_s, t_mix_s, small, sems,
):
    z, core, x = pos[0], pos[1], pos[2]
    first = [begin(dirs, dirs_s, small.at[1])]
    for k in range(NZ):
        begin(rows.at[k], rows_s.at[k], sems.at[k])
    second = [
        begin(got.at[pl.ds(z, 1)], got_s, small.at[2]),
        begin(s_mix, s_mix_s, small.at[3]),
        begin(t_mix, t_mix_s, small.at[4]),
        begin(student_part, part_s, small.at[5]),
    ]
    acc_s[...] = jnp.zeros_like(acc_s)
    for copy in first:
        copy.wait()

    @pl.loop(0, NZ, unroll=2)
    def _(k):
        total = jnp.sum(stat[pos[3 + k]], axis=0)
        scale = down_rows(FACTOR / lanes512(total))
        pltpu.make_async_copy(rows.at[k], rows_s.at[k], sems.at[k]).wait()
        expo = jnp.exp2(dot(dirs_s[...], rows_s[k, :, :DIM], NT) * T_EXP2).astype(bf16)
        r = scale_rows(rows_s[k, :, DIM:].astype(f32), scale).astype(bf16)
        acc_s[...] += dot(expo, r, NN)

    for copy in second:
        copy.wait()
    for d in range(NX):
        i = lax.rem(x + d, NX)
        c = col[pl.ds(2 * i + z // 4, 1), :]
        c = sum(jnp.where(lax.rem(z, 4) == q, c[:, q * DIM : (q + 1) * DIM], 0.0) for q in range(4))
        part = pl.ds(pl.multiple_of(i * DIM, DIM), DIM)
        block = part_s[part, :] - scale_rows(acc_s[part, :], down_rows(c))
        if d == 0:
            own_o[...] = block
        else:
            (next1_o, next2_o, next3_o)[d - 1][...] = block.astype(bf16)

    row_total = lanes512(jnp.sum(stat[z], axis=0))
    total = got_s[0].astype(f32)[:, BK:]
    total = lanes512(total[:4] + total[4:])
    s_mix_s[...] = scale_rows(s_mix_s[...], down_rows(FACTOR / total)) - scale_rows(
        t_mix_s[...], down_rows(FACTOR / row_total)
    )
    half = ROWS // NC
    keep_o[:half, :] = s_mix_s[pl.ds(pl.multiple_of(core * half, half), half), :]
    give_o[:half, :] = s_mix_s[pl.ds(pl.multiple_of((1 - core) * half, half), half), :].astype(bf16)
    loss = cross[...] / row_total
    low, high = loss[:, :half], loss[:, half:]
    away = jnp.where(core == 0, high, low)
    hi = away.astype(bf16).astype(f32)
    zeros = jnp.zeros((14, DIM), f32)
    give_o[half:, :] = jnp.concatenate([hi, away - hi, zeros], axis=0).astype(bf16)
    keep_o[half:, :] = jnp.concatenate([jnp.where(core == 0, low, high), zeros[:7]], axis=0)
    line_o[...] = jnp.log(total)


def proto_part(pos, dirs, rows, stat, got, student_part, col, s_mix, t_mix, cross):
    n, half = NX * DIM, ROWS // NC
    return call(
        grad_kernel,
        [SCALARS, ANY, ANY, INSIDE, ANY, ANY, INSIDE, ANY, ANY, INSIDE],
        [INSIDE] * 7,
        [
            shape((DIM, DIM), f32),
            shape((DIM, DIM), bf16),
            shape((DIM, DIM), bf16),
            shape((DIM, DIM), bf16),
            shape((half + 8, DIM), f32),
            shape((half + 16, DIM), bf16),
            shape((1, ROWS), f32),
        ],
        [
            pltpu.VMEM((NZ, ROWS, 2 * DIM), bf16),
            pltpu.VMEM((1,) + got.shape[1:], bf16),
            pltpu.VMEM((n, DIM), bf16),
            pltpu.VMEM((n, DIM), f32),
            pltpu.VMEM((n, DIM), f32),
            pltpu.VMEM((ROWS, DIM), f32),
            pltpu.VMEM((ROWS, DIM), f32),
            DMA((6,)),
            DMA((NZ,)),
        ],
        4 * ROWS * COLS * DIM,
        ROWS * COLS,
        "proto_part",
        MIDDLE,
    )(pos, dirs, rows, stat, got, student_part, col, s_mix, t_mix, cross)


def gather(a, axes):
    return lax.all_to_all(a, axes, 0, 0)


def swap_core(a):
    return lax.ppermute(a, "c", [(0, 1), (1, 0)])


def shift(a, axis, by):
    n = lax.axis_size(axis)
    return lax.ppermute(a, axis, [(i, (i + by) % n) for i in range(n)])


OFFSETS = (0, -1, 1, -2, 2, -3, 3, -4)


def packed(terms, loss):
    hi = lax.reduce_precision(loss, 8, 7)
    tail = jnp.concatenate([hi, loss - hi, jnp.zeros((14, DIM), f32)], axis=0)
    return jnp.concatenate([terms, tail], axis=0).astype(bf16)


def unpacked(a):
    a = a.astype(f32)
    n = a.shape[0] - 16
    return a[:n], a[n : n + 1] + a[n + 1 : n + 2]


def around(a, axis):
    one, two, three = [shift(a, axis, d).astype(f32) for d in (1, 2, 3)]
    return (a.astype(f32) + two) + (one + three)


def local(teacher_feat, student_feat, teacher_protos, student_protos):
    z = lax.axis_index("z")
    core = lax.axis_index("c")
    half = ROWS // NC
    together = lax.optimization_barrier

    def my_half(a):
        return lax.dynamic_slice_in_dim(a, core * half, half, 0)

    order = (z + jnp.array(OFFSETS, jnp.int32)) % NZ
    pos = jnp.concatenate([jnp.stack([z, core, lax.axis_index("x")]), order]).astype(jnp.int32)

    b0 = jnp.concatenate([my_half(teacher_feat), my_half(student_feat)], axis=1)
    u1, d1 = shift(b0, "z", 1), shift(b0, "z", -1)
    expo, cols = teacher(teacher_feat, teacher_protos)
    cols, u1, d1 = together((cols, u1, d1))

    u2, d2 = shift(u1, "z", 1), shift(d1, "z", -1)
    o0, ou1, od1 = swap_core(b0), swap_core(u1), swap_core(d1)
    got = gather(cols, ("x", "z"))
    s_dirs, tot, s_mix = student(student_feat, student_protos)
    got, u2, d2, o0, ou1, od1, tot = together((got, u2, d2, o0, ou1, od1, tot))

    u3, d3 = shift(u2, "z", 1), shift(d2, "z", -1)
    ou2, od2 = swap_core(u2), swap_core(d2)
    rows = row_pass(expo, got, tot)
    rows, u3, d3, ou2, od2 = together((rows, u3, d3, ou2, od2))
    u4 = shift(u3, "z", 1)
    got = gather(rows, ("y", "c"))
    got, u4 = together((got, u4))

    cols, tots = col_pass(expo, got, 1)
    cols = around(cols[0], "x").astype(bf16)
    cols = jnp.concatenate([cols, tots], axis=1)
    got2 = gather(jnp.broadcast_to(cols[None], (NZ,) + cols.shape), "z")

    got2, u3, d3, u4 = together((got2, u3, d3, u4))
    ou3, od3, ou4 = swap_core(u3), swap_core(d3), swap_core(u4)
    rows = row_pass(expo, got2, tot)
    rows, ou3, od3, ou4 = together((rows, ou3, od3, ou4))
    got = gather(rows, ("y", "c"))
    cols, _ = col_pass(expo, got, NX * NZ)

    got = gather(cols, ("x", "z"))
    rows_c, dirs_c, student_part = early(
        pos,
        [b0, u1, d1, u2, d2, u3, d3, u4],
        [o0, ou1, od1, ou2, od2, ou3, od3, ou4],
        teacher_protos.reshape(NX, NZ, DIM, DIM),
        s_dirs.reshape(NX, NZ, DIM, DIM),
        got2,
    )
    got, student_part = together((got, student_part))

    rows, col = row_last(expo, got)
    rows, col = together((rows, col))
    stat = gather(rows, ("z", "y", "c")).reshape(NZ, NY * NC, 4, 128)
    t_mix, cross = mix_pass(expo, col, s_dirs, student_feat)
    stat, t_mix, cross = together((stat, t_mix, cross))
    own, next1, next2, next3, keep, give, log_total = proto_part(
        pos, dirs_c, rows_c, stat, got2, student_part, col, s_mix, t_mix, cross
    )
    arrived = [shift(a, "x", d).astype(f32) for a, d in ((next1, 1), (next2, 2), (next3, 3))]
    proto_grad = ((own + arrived[0]) + (arrived[1] + arrived[2])).astype(bf16)

    terms, loss = unpacked(swap_core(give))
    mine = packed(keep[:half] + terms, keep[half : half + 1] + loss)
    terms, loss = unpacked(mine)
    away = [unpacked(shift(mine, "y", d)) for d in (1, 2, 3)]
    terms = (terms + away[1][0]) + (away[0][0] + away[2][0])
    loss = (loss + away[1][1]) + (away[0][1] + away[2][1])
    done = packed(terms, loss)
    there = swap_core(done)
    low, low_loss = unpacked(jnp.where(core == 0, done, there))
    high, high_loss = unpacked(jnp.where(core == 0, there, done))
    feature_grad = jnp.concatenate([low, high], axis=0).astype(bf16)
    row_loss = (log_total - jnp.concatenate([low_loss, high_loss], axis=1)).reshape(ROWS)
    return row_loss, feature_grad, proto_grad


def solution(mesh):
    fine = Mesh(mesh.devices.reshape(NX, NZ, NY, NC), ("x", "z", "y", "c"))
    rows, protos = P(("x", "z"), None), P(("y", "c"), None)
    return jax.shard_map(
        local,
        mesh=fine,
        in_specs=(rows, rows, protos, protos),
        out_specs=(P(("x", "z")), rows, P(("y", "c", "x", "z"), None)),
        check_vma=False,
    )
```

profile of v0, /device:TPU:1, one launch (start us, length us, event | category | flops | bytes accessed | tf_op | source)
XLA Modules:
  0.0 178.4 jit_solution(9410466601945595024)
XLA Ops:
  0.6 1.0 constant_dynamic-slice_fusion
  1.7 2.5 %collective-permute-start = (bf16[256,512]{1,0:T(8,128)(2,1)S(1)}, bf16[256,512]{1,0:T(8,128)(2,1)S(1)}, u32[]{:S(2)}, u32[]{:S(2)}) collective-permute-start(bf16[256,512]{1,0:T(8,128)(2,1)S(1)} %pad_maximum_fusion.refs_1_), channel_id=1, source_target_pairs={{0,8},{8,16},{16,24},{24,32},{32,40},{40,48},{48,56},{56,0},{1,9},... | collective-permute-start | bytes 786440 | tf_op jit(solution)/shard_map/ppermute | solution.py:513
  4.2 4.0 %collective-permute-start.1 = (bf16[256,512]{1,0:T(8,128)(2,1)S(1)}, bf16[256,512]{1,0:T(8,128)(2,1)S(1)}, u32[]{:S(2)}, u32[]{:S(2)}) collective-permute-start(bf16[256,512]{1,0:T(8,128)(2,1)S(1)} %pad_maximum_fusion.refs_1_), channel_id=1, source_target_pairs={{0,56},{8,0},{16,8},{24,16},{32,24},{40,32},{48,40},{56,48},{1,57}... | collective-permute-start | bytes 786440 | tf_op jit(solution)/shard_map/ppermute | solution.py:513
  8.2 9.0 %teacher.1 = (bf16[8,512,1024]{2,1,0:T(8,128)(2,1)}, bf16[32,8,1024]{2,1,0:T(8,128)(2,1)}) custom-call(bf16[512,256]{1,0:T(8,128)(2,1)} %feat.3, bf16[8,1024,256]{2,1,0:T(8,128)(2,1)} %bitcast.18), custom_call_target="tpu_custom_call" | custom-call | flops 2147483648 | bytes 12582912 | tf_op jit(solution)/shard_map/teacher/pallas_call | solution.py:122
  17.3 8.1 %all-to-all-start = ((bf16[32,8,1024]{2,1,0:T(8,128)(2,1)}), bf16[32,8,1024]{2,1,0:T(8,128)(2,1)S(1)}, u32[]{:S(2)}, u32[]{:S(2)}) async-start(bf16[32,8,1024]{2,1,0:T(8,128)(2,1)} %get-tuple-element.58), calls=%async_computation | async-start | bytes 1048576 | tf_op jit(solution)/shard_map/all_to_all | solution.py:504
  25.3 1.6 collective-permute-start.4
  26.9 1.5 collective-permute-start.2
  28.8 1.2 collective-permute-start.3
  30.5 10.7 %student.1 = (bf16[8,1024,256]{2,1,0:T(8,128)(2,1)}, f32[4,128]{1,0:T(4,128)}, f32[512,256]{1,0:T(8,128)}) custom-call(bf16[512,256]{1,0:T(8,128)(2,1)} %feat.5, bf16[8,1024,256]{2,1,0:T(8,128)(2,1)} %bitcast.17), custom_call_target="tpu_custom_call" | custom-call | flops 4294967296 | bytes 8388608 | tf_op jit(solution)/shard_map/student/pallas_call | solution.py:174
  41.2 3.5 %collective-permute-done.2.refs_4_ = bf16[256,512]{1,0:T(8,128)(2,1)S(1)} collective-permute-done((bf16[256,512]{1,0:T(8,128)(2,1)S(1)}, bf16[256,512]{1,0:T(8,128)(2,1)S(1)}, u32[]{:S(2)}, u32[]{:S(2)}) %collective-permute-start.2) | collective-permute-done | bytes 262176 | tf_op jit(solution)/shard_map/ppermute | solution.py:513
  45.0 2.5 %collective-permute-start.8 = (bf16[256,512]{1,0:T(8,128)(2,1)S(1)}, bf16[256,512]{1,0:T(8,128)(2,1)S(1)}, u32[]{:S(2)}, u32[]{:S(2)}) collective-permute-start(bf16[256,512]{1,0:T(8,128)(2,1)S(1)} %collective-permute-done.3.refs_5_), channel_id=1, source_target_pairs={{0,56},{8,0},{16,8},{24,16},{32,24},{40,32},{48,40},{56,48},{1,57}... | collective-permute-start | bytes 786440 | tf_op jit(solution)/shard_map/ppermute | solution.py:513
  47.5 2.3 %collective-permute-start.9 = (bf16[256,512]{1,0:T(8,128)(2,1)S(1)}, bf16[256,512]{1,0:T(8,128)(2,1)S(1)}, u32[]{:S(2)}, u32[]{:S(2)}) collective-permute-start(bf16[256,512]{1,0:T(8,128)(2,1)S(1)} %collective-permute-done.2.refs_4_), channel_id=1, source_target_pairs={{0,1},{1,0},{2,3},{3,2},{4,5},{5,4},{6,7},{7,6},{8,9},{9,8},{10,11... | collective-permute-start | bytes 786440 | tf_op jit(solution)/shard_map/ppermute | solution.py:508
  49.7 3.4 %copy-done = bf16[8,512,1024]{2,1,0:T(8,128)(2,1)S(1)} copy-done((bf16[8,512,1024]{2,1,0:T(8,128)(2,1)S(1)}, bf16[8,512,1024]{2,1,0:T(8,128)(2,1)}, u32[]{:S(2)}) %copy-start) | copy-done | bytes 8388632
  53.1 0.7 copy-done.7
  53.8 1.9 %row_pass.2 = f32[8,8,128]{2,1,0:T(8,128)S(1)} custom-call(bf16[8,512,1024]{2,1,0:T(8,128)(2,1)S(1)} %copy-done, bf16[32,8,1024]{2,1,0:T(8,128)(2,1)S(1)} %all-to-all-done.got, f32[4,128]{1,0:T(4,128)S(1)} %copy-done.7), custom_call_target="tpu_custom_call" | custom-call | flops 8388608 | bytes 65536 | tf_op jit(solution)/shard_map/row_pass/pallas_call | solution.py:230
  56.1 9.6 %all_to_all.30.got = f32[8,8,128]{2,1,0:T(8,128)S(1)} all-to-all(f32[8,8,128]{2,1,0:T(8,128)S(1)} %row_pass.2), channel_id=1, replica_groups=mesh['x'=4,'z'=8,'y'=4,'c'=2] {'y','c'}, dimensions={0} | all-to-all | bytes 65536 | tf_op jit(solution)/shard_map/all_to_all | solution.py:504
  65.8 1.9 %col_pass.2 = (bf16[1,8,1024]{2,1,0:T(8,128)(2,1)S(1)}, bf16[8,128]{1,0:T(8,128)(2,1)S(1)}) custom-call(bf16[8,512,1024]{2,1,0:T(8,128)(2,1)S(1)} %copy-done.1, f32[8,8,128]{2,1,0:T(8,128)S(1)} %all_to_all.30.got), custom_call_target="tpu_custom_call" | custom-call | flops 8388608 | bytes 1048576 | tf_op jit(solution)/shard_map/col_pass/pallas_call | solution.py:284
  67.7 2.6 %collective-permute-start.14 = (bf16[8,1024]{1,0:T(8,128)(2,1)S(1)}, bf16[8,1024]{1,0:T(8,128)(2,1)S(1)}, u32[]{:S(2)}, u32[]{:S(2)}) collective-permute-start(bf16[8,1024]{1,0:T(8,128)(2,1)S(1)} %bitcast.12), channel_id=1, source_target_pairs={{0,192},{64,0},{128,64},{192,128},{1,193},{65,1},{129,65},{193,129... | collective-permute-start | bytes 49160 | tf_op jit(solution)/shard_map/ppermute | solution.py:513
  70.3 1.7 collective-permute-start.12
  72.0 2.1 %collective-permute-done.13 = bf16[8,1024]{1,0:T(8,128)(2,1)S(1)} collective-permute-done((bf16[8,1024]{1,0:T(8,128)(2,1)S(1)}, bf16[8,1024]{1,0:T(8,128)(2,1)S(1)}, u32[]{:S(2)}, u32[]{:S(2)}) %collective-permute-start.13) | collective-permute-done | bytes 16416 | tf_op jit(solution)/shard_map/ppermute | solution.py:513
  74.4 12.6 %all_to_all.31.got.refs_19_ = bf16[8,8,1152]{2,1,0:T(8,128)(2,1)S(1)} all-to-all(bf16[8,8,1152]{2,1,0:T(8,128)(2,1)S(1)} %broadcast_in_dim.2), channel_id=1, replica_groups=mesh['x'=4,'z'=8,'y'=4,'c'=2] {'z'}, dimensions={0} | all-to-all | bytes 294912 | tf_op jit(solution)/shard_map/all_to_all | solution.py:504
  87.1 3.5 %collective-permute-start.15 = (bf16[256,512]{1,0:T(8,128)(2,1)S(1)}, bf16[256,512]{1,0:T(8,128)(2,1)S(1)}, u32[]{:S(2)}, u32[]{:S(2)}) collective-permute-start(bf16[256,512]{1,0:T(8,128)(2,1)S(1)} %collective-permute-done.7.refs_6_), channel_id=1, source_target_pairs={{0,1},{1,0},{2,3},{3,2},{4,5},{5,4},{6,7},{7,6},{8,9},{9,8},{10,11... | collective-permute-start | bytes 786440 | tf_op jit(solution)/shard_map/ppermute | solution.py:508
  91.1 1.9 %row_pass.3 = f32[8,8,128]{2,1,0:T(8,128)S(1)} custom-call(bf16[8,512,1024]{2,1,0:T(8,128)(2,1)S(1)} %copy-done.1, bf16[8,8,1152]{2,1,0:T(8,128)(2,1)S(1)} %all_to_all.31.got.refs_19_, f32[4,128]{1,0:T(4,128)S(1)} %copy-done.7), custom_call_target="tpu_custom_call" | custom-call | flops 8388608 | bytes 65536 | tf_op jit(solution)/shard_map/row_pass/pallas_call | solution.py:230
  93.0 8.3 %all_to_all.32.got = f32[8,8,128]{2,1,0:T(8,128)S(1)} all-to-all(f32[8,8,128]{2,1,0:T(8,128)S(1)} %row_pass.3), channel_id=1, replica_groups=mesh['x'=4,'z'=8,'y'=4,'c'=2] {'y','c'}, dimensions={0} | all-to-all | bytes 65536 | tf_op jit(solution)/shard_map/all_to_all | solution.py:504
  101.3 2.8 %col_pass.3 = (bf16[32,8,1024]{2,1,0:T(8,128)(2,1)}, bf16[8,128]{1,0:T(8,128)(2,1)}) custom-call(bf16[8,512,1024]{2,1,0:T(8,128)(2,1)S(1)} %copy-done.1, f32[8,8,128]{2,1,0:T(8,128)S(1)} %all_to_all.32.got), custom_call_target="tpu_custom_call" | custom-call | flops 8388608 | bytes 1048576 | tf_op jit(solution)/shard_map/col_pass/pallas_call | solution.py:284
  104.1 4.6 %all-to-all-start.4 = ((bf16[32,8,1024]{2,1,0:T(8,128)(2,1)}), bf16[32,8,1024]{2,1,0:T(8,128)(2,1)S(1)}, u32[]{:S(2)}, u32[]{:S(2)}) async-start(bf16[32,8,1024]{2,1,0:T(8,128)(2,1)} %get-tuple-element.88), calls=%async_computation.4 | async-start | bytes 1048576 | tf_op jit(solution)/shard_map/all_to_all | solution.py:504
  108.8 0.7 pad_add_fusion.refs_0_.pos
  109.4 13.1 %early.1 = (bf16[8,512,512]{2,1,0:T(8,128)(2,1)}, bf16[1024,256]{1,0:T(8,128)(2,1)}, f32[1024,256]{1,0:T(8,128)}) custom-call(s32[11]{0:T(128)} %pad_add_fusion.refs_0_.pos, bf16[256,512]{1,0:T(8,128)(2,1)} %copy-done.14, bf16[256,512]{1,0:T(8,128)(2,1)} %copy-done.15, bf16[256,512]{1,0:T(8,128)(2,1)} %copy-done.16, bf16[256,512]{1,0:T(8,128)(2,1)} %copy-done.18, ...), custom_call_target="tpu_custom_call" | custom-call | flops 4294967296 | bytes 4194304 | tf_op jit(solution)/shard_map/early/pallas_call | solution.py:380
  122.9 3.4 %copy-done.2 = bf16[8,512,1024]{2,1,0:T(8,128)(2,1)S(1)} copy-done((bf16[8,512,1024]{2,1,0:T(8,128)(2,1)S(1)}, bf16[8,512,1024]{2,1,0:T(8,128)(2,1)}, u32[]{:S(2)}) %copy-start.2) | copy-done | bytes 8388632
  126.3 2.6 %row_last.1 = (f32[64,4,128]{2,1,0:T(4,128)}, f32[8,1024]{1,0:T(8,128)S(1)}) custom-call(bf16[8,512,1024]{2,1,0:T(8,128)(2,1)S(1)} %copy-done.2, bf16[32,8,1024]{2,1,0:T(8,128)(2,1)S(1)} %all-to-all-done.4.got), custom_call_target="tpu_custom_call" | custom-call | flops 8388608 | bytes 65536 | tf_op jit(solution)/shard_map/row_last/pallas_call | solution.py:249
  129.5 9.2 %all-to-all-start.5 = ((f32[64,4,128]{2,1,0:T(4,128)}), f32[64,4,128]{2,1,0:T(4,128)S(1)}, u32[]{:S(2)}, u32[]{:S(2)}) async-start(f32[64,4,128]{2,1,0:T(4,128)} %get-tuple-element.91), calls=%async_computation.5 | async-start | bytes 262144 | tf_op jit(solution)/shard_map/all_to_all | solution.py:504
  138.8 8.3 %mix_pass.1 = (f32[512,256]{1,0:T(8,128)}, f32[1,512]{1,0:T(1,128)}) custom-call(bf16[8,512,1024]{2,1,0:T(8,128)(2,1)} %get-tuple-element.62.expo, f32[8,1024]{1,0:T(8,128)} %copy-done.5, bf16[8,1024,256]{2,1,0:T(8,128)(2,1)} %get-tuple-element.84.dirs, bf16[512,256]{1,0:T(8,128)(2,1)} %feat.5), custom_call_target="tpu_custom_call" | custom-call | flops 2147483648 | bytes 12582912 | tf_op jit(solution)/shard_map/mix_pass/pallas_call | solution.py:322
  147.1 2.7 %all-to-all-done.5 = f32[64,4,128]{2,1,0:T(4,128)S(1)} async-done(((f32[64,4,128]{2,1,0:T(4,128)}), f32[64,4,128]{2,1,0:T(4,128)S(1)}, u32[]{:S(2)}, u32[]{:S(2)}) %all-to-all-start.5) | async-done | bytes 131104 | tf_op jit(solution)/shard_map/all_to_all | solution.py:504
  149.9 1.0 copy-done.9
  150.9 0.7 copy-done.10
  151.6 9.0 %proto_part.1 = (f32[256,256]{1,0:T(8,128)S(1)}, bf16[256,256]{1,0:T(8,128)(2,1)S(1)}, bf16[256,256]{1,0:T(8,128)(2,1)S(1)}, bf16[256,256]{1,0:T(8,128)(2,1)S(1)...) custom-call(s32[11]{0:T(128)S(1)} %copy-done.8, bf16[1024,256]{1,0:T(8,128)(2,1)S(1)} %copy-done.12, ...), custom_call_target="tpu_custom_call" | custom-call | flops 4294967296 | bytes 4194304 | tf_op jit(solution)/shard_map/proto_part/pallas_call | solution.py:472
  160.6 0.7 collective-permute-start.18
  161.4 0.9 collective-permute-done.18
  162.5 0.7 collective-permute-start.21
  163.2 0.9 collective-permute-start.20
  164.0 1.2 collective-permute-start.19
  165.2 2.0 %collective-permute-start.25 = (bf16[256,256]{1,0:T(8,128)(2,1)S(1)}, bf16[256,256]{1,0:T(8,128)(2,1)S(1)}, u32[]{:S(2)}, u32[]{:S(2)}) collective-permute-start(bf16[256,256]{1,0:T(8,128)(2,1)S(1)} %get-tuple-element.106), channel_id=1, source_target_pairs={{0,192},{64,0},{128,64},{192,128},{1,193},{65,1},{129,65},{193,129... | collective-permute-start | bytes 393224 | tf_op jit(solution)/shard_map/ppermute | solution.py:513
  168.4 1.2 collective-permute-done.20
  169.5 1.8 collective-permute-done.19
  171.6 2.2 %collective-permute-start.22 = (bf16[272,256]{1,0:T(8,128)(2,1)S(1)}, bf16[272,256]{1,0:T(8,128)(2,1)S(1)}, u32[]{:S(2)}, u32[]{:S(2)}) collective-permute-start(bf16[272,256]{1,0:T(8,128)(2,1)S(1)} %maximum_maximum_fusion.1), channel_id=1, source_target_pairs={{0,1},{1,0},{2,3},{3,2},{4,5},{5,4},{6,7},{7,6},{8,9},{9,8},{10,11... | collective-permute-start | bytes 417800 | tf_op jit(solution)/shard_map/ppermute | solution.py:508
  173.8 2.4 %collective-permute-done.23 = bf16[256,256]{1,0:T(8,128)(2,1)S(1)} collective-permute-done((bf16[256,256]{1,0:T(8,128)(2,1)S(1)}, bf16[256,256]{1,0:T(8,128)(2,1)S(1)}, u32[]{:S(2)}, u32[]{:S(2)}) %collective-permute-start.23) | collective-permute-done | bytes 131104 | tf_op jit(solution)/shard_map/ppermute | solution.py:513
  176.2 0.7 add_convert_fusion
  177.1 0.7 pad_maximum_fusion.1
  (114 shorter events, 5.8 us)
Async XLA Ops:
  1.7 23.7 %copy-start.14 = (bf16[256,512]{1,0:T(8,128)(2,1)}, bf16[256,512]{1,0:T(8,128)(2,1)S(1)}, u32[]{:S(2)}) copy-start(bf16[256,512]{1,0:T(8,128)(2,1)S(1)} %pad_maximum_fusion.refs_1_) | copy-start | bytes 786436
  1.7 15.6 %collective-permute-start = (bf16[256,512]{1,0:T(8,128)(2,1)S(1)}, bf16[256,512]{1,0:T(8,128)(2,1)S(1)}, u32[]{:S(2)}, u32[]{:S(2)}) collective-permute-start(bf16[256,512]{1,0:T(8,128)(2,1)S(1)} %pad_maximum_fusion.refs_1_), channel_id=1, source_target_pairs={{0,8},{8,16},{16,24},{24,32},{32,40},{40,48},{48,56},{56,0},{1,9},... | collective-permute-start | bytes 786440 | tf_op jit(solution)/shard_map/ppermute | solution.py:513
  4.2 13.0 %collective-permute-start.1 = (bf16[256,512]{1,0:T(8,128)(2,1)S(1)}, bf16[256,512]{1,0:T(8,128)(2,1)S(1)}, u32[]{:S(2)}, u32[]{:S(2)}) collective-permute-start(bf16[256,512]{1,0:T(8,128)(2,1)S(1)} %pad_maximum_fusion.refs_1_), channel_id=1, source_target_pairs={{0,56},{8,0},{16,8},{24,16},{32,24},{40,32},{48,40},{56,48},{1,57}... | collective-permute-start | bytes 786440 | tf_op jit(solution)/shard_map/ppermute | solution.py:513
  17.2 23.9 %copy-start.15 = (bf16[256,512]{1,0:T(8,128)(2,1)}, bf16[256,512]{1,0:T(8,128)(2,1)S(1)}, u32[]{:S(2)}) copy-start(bf16[256,512]{1,0:T(8,128)(2,1)S(1)} %collective-permute-done.refs_2_) | copy-start | bytes 786436
  17.2 23.9 %copy-start.16 = (bf16[256,512]{1,0:T(8,128)(2,1)}, bf16[256,512]{1,0:T(8,128)(2,1)S(1)}, u32[]{:S(2)}) copy-start(bf16[256,512]{1,0:T(8,128)(2,1)S(1)} %collective-permute-done.1.refs_3_) | copy-start | bytes 786436
  17.3 27.4 %all-to-all-start = ((bf16[32,8,1024]{2,1,0:T(8,128)(2,1)}), bf16[32,8,1024]{2,1,0:T(8,128)(2,1)S(1)}, u32[]{:S(2)}, u32[]{:S(2)}) async-start(bf16[32,8,1024]{2,1,0:T(8,128)(2,1)} %get-tuple-element.58), calls=%async_computation | async-start | bytes 1048576 | tf_op jit(solution)/shard_map/all_to_all | solution.py:504
  25.3 15.8 %collective-permute-start.4 = (bf16[256,512]{1,0:T(8,128)(2,1)S(1)}, bf16[256,512]{1,0:T(8,128)(2,1)S(1)}, u32[]{:S(2)}, u32[]{:S(2)}) collective-permute-start(bf16[256,512]{1,0:T(8,128)(2,1)S(1)} %pad_maximum_fusion.refs_1_), channel_id=1, source_target_pairs={{0,1},{1,0},{2,3},{3,2},{4,5},{5,4},{6,7},{7,6},{8,9},{9,8},{10,11... | collective-permute-start | bytes 786440 | tf_op jit(solution)/shard_map/ppermute | solution.py:508
  26.9 17.7 %collective-permute-start.2 = (bf16[256,512]{1,0:T(8,128)(2,1)S(1)}, bf16[256,512]{1,0:T(8,128)(2,1)S(1)}, u32[]{:S(2)}, u32[]{:S(2)}) collective-permute-start(bf16[256,512]{1,0:T(8,128)(2,1)S(1)} %collective-permute-done.refs_2_), channel_id=1, source_target_pairs={{0,8},{8,16},{16,24},{24,32},{32,40},{40,48},{48,56},{56,0},{1,9},... | collective-permute-start | bytes 786440 | tf_op jit(solution)/shard_map/ppermute | solution.py:513
  28.5 16.2 %collective-permute-start.5 = (bf16[256,512]{1,0:T(8,128)(2,1)S(1)}, bf16[256,512]{1,0:T(8,128)(2,1)S(1)}, u32[]{:S(2)}, u32[]{:S(2)}) collective-permute-start(bf16[256,512]{1,0:T(8,128)(2,1)S(1)} %collective-permute-done.refs_2_), channel_id=1, source_target_pairs={{0,1},{1,0},{2,3},{3,2},{4,5},{5,4},{6,7},{7,6},{8,9},{9,8},{10,11... | collective-permute-start | bytes 786440 | tf_op jit(solution)/shard_map/ppermute | solution.py:508
  28.8 15.8 %collective-permute-start.3 = (bf16[256,512]{1,0:T(8,128)(2,1)S(1)}, bf16[256,512]{1,0:T(8,128)(2,1)S(1)}, u32[]{:S(2)}, u32[]{:S(2)}) collective-permute-start(bf16[256,512]{1,0:T(8,128)(2,1)S(1)} %collective-permute-done.1.refs_3_), channel_id=1, source_target_pairs={{0,56},{8,0},{16,8},{24,16},{32,24},{40,32},{48,40},{56,48},{1,57}... | collective-permute-start | bytes 786440 | tf_op jit(solution)/shard_map/ppermute | solution.py:513
  30.0 14.7 %collective-permute-start.6 = (bf16[256,512]{1,0:T(8,128)(2,1)S(1)}, bf16[256,512]{1,0:T(8,128)(2,1)S(1)}, u32[]{:S(2)}, u32[]{:S(2)}) collective-permute-start(bf16[256,512]{1,0:T(8,128)(2,1)S(1)} %collective-permute-done.1.refs_3_), channel_id=1, source_target_pairs={{0,1},{1,0},{2,3},{3,2},{4,5},{5,4},{6,7},{7,6},{8,9},{9,8},{10,11... | collective-permute-start | bytes 786440 | tf_op jit(solution)/shard_map/ppermute | solution.py:508
  41.1 14.6 %copy-start.17 = (bf16[256,512]{1,0:T(8,128)(2,1)}, bf16[256,512]{1,0:T(8,128)(2,1)S(1)}, u32[]{:S(2)}) copy-start(bf16[256,512]{1,0:T(8,128)(2,1)S(1)} %collective-permute-done.4.refs_9_) | copy-start | bytes 786436
  44.6 11.1 %copy-start.18 = (bf16[256,512]{1,0:T(8,128)(2,1)}, bf16[256,512]{1,0:T(8,128)(2,1)S(1)}, u32[]{:S(2)}) copy-start(bf16[256,512]{1,0:T(8,128)(2,1)S(1)} %collective-permute-done.2.refs_4_) | copy-start | bytes 786436
  44.6 11.1 %copy-start.20 = (bf16[256,512]{1,0:T(8,128)(2,1)}, bf16[256,512]{1,0:T(8,128)(2,1)S(1)}, u32[]{:S(2)}) copy-start(bf16[256,512]{1,0:T(8,128)(2,1)S(1)} %collective-permute-done.3.refs_5_) | copy-start | bytes 786436
  44.7 11.1 %copy-start.19 = (bf16[256,512]{1,0:T(8,128)(2,1)}, bf16[256,512]{1,0:T(8,128)(2,1)S(1)}, u32[]{:S(2)}) copy-start(bf16[256,512]{1,0:T(8,128)(2,1)S(1)} %collective-permute-done.5.refs_10_) | copy-start | bytes 786436
  44.7 11.1 %copy-start.21 = (bf16[256,512]{1,0:T(8,128)(2,1)}, bf16[256,512]{1,0:T(8,128)(2,1)S(1)}, u32[]{:S(2)}) copy-start(bf16[256,512]{1,0:T(8,128)(2,1)S(1)} %collective-permute-done.6.refs_11_) | copy-start | bytes 786436
  44.7 11.1 %collective-permute-start.7 = (bf16[256,512]{1,0:T(8,128)(2,1)S(1)}, bf16[256,512]{1,0:T(8,128)(2,1)S(1)}, u32[]{:S(2)}, u32[]{:S(2)}) collective-permute-start(bf16[256,512]{1,0:T(8,128)(2,1)S(1)} %collective-permute-done.2.refs_4_), channel_id=1, source_target_pairs={{0,8},{8,16},{16,24},{24,32},{32,40},{40,48},{48,56},{56,0},{1,9},... | collective-permute-start | bytes 786440 | tf_op jit(solution)/shard_map/ppermute | solution.py:513
  45.0 10.8 %collective-permute-start.8 = (bf16[256,512]{1,0:T(8,128)(2,1)S(1)}, bf16[256,512]{1,0:T(8,128)(2,1)S(1)}, u32[]{:S(2)}, u32[]{:S(2)}) collective-permute-start(bf16[256,512]{1,0:T(8,128)(2,1)S(1)} %collective-permute-done.3.refs_5_), channel_id=1, source_target_pairs={{0,56},{8,0},{16,8},{24,16},{32,24},{40,32},{48,40},{56,48},{1,57}... | collective-permute-start | bytes 786440 | tf_op jit(solution)/shard_map/ppermute | solution.py:513
  47.5 8.4 %collective-permute-start.9 = (bf16[256,512]{1,0:T(8,128)(2,1)S(1)}, bf16[256,512]{1,0:T(8,128)(2,1)S(1)}, u32[]{:S(2)}, u32[]{:S(2)}) collective-permute-start(bf16[256,512]{1,0:T(8,128)(2,1)S(1)} %collective-permute-done.2.refs_4_), channel_id=1, source_target_pairs={{0,1},{1,0},{2,3},{3,2},{4,5},{5,4},{6,7},{7,6},{8,9},{9,8},{10,11... | collective-permute-start | bytes 786440 | tf_op jit(solution)/shard_map/ppermute | solution.py:508
  49.7 6.1 %collective-permute-start.10 = (bf16[256,512]{1,0:T(8,128)(2,1)S(1)}, bf16[256,512]{1,0:T(8,128)(2,1)S(1)}, u32[]{:S(2)}, u32[]{:S(2)}) collective-permute-start(bf16[256,512]{1,0:T(8,128)(2,1)S(1)} %collective-permute-done.3.refs_5_), channel_id=1, source_target_pairs={{0,1},{1,0},{2,3},{3,2},{4,5},{5,4},{6,7},{7,6},{8,9},{9,8},{10,11... | collective-permute-start | bytes 786440 | tf_op jit(solution)/shard_map/ppermute | solution.py:508
  53.8 12.0 %copy-start.1 = (bf16[8,512,1024]{2,1,0:T(8,128)(2,1)S(1)}, bf16[8,512,1024]{2,1,0:T(8,128)(2,1)}, u32[]{:S(2)}) copy-start(bf16[8,512,1024]{2,1,0:T(8,128)(2,1)} %get-tuple-element.62.expo) | copy-start | bytes 25165828
  55.8 31.2 %copy-start.22 = (bf16[256,512]{1,0:T(8,128)(2,1)}, bf16[256,512]{1,0:T(8,128)(2,1)S(1)}, u32[]{:S(2)}) copy-start(bf16[256,512]{1,0:T(8,128)(2,1)S(1)} %collective-permute-done.7.refs_6_) | copy-start | bytes 786436
  55.8 34.7 %copy-start.23 = (bf16[256,512]{1,0:T(8,128)(2,1)}, bf16[256,512]{1,0:T(8,128)(2,1)S(1)}, u32[]{:S(2)}) copy-start(bf16[256,512]{1,0:T(8,128)(2,1)S(1)} %collective-permute-done.8.refs_7_) | copy-start | bytes 786436
  55.8 11.8 %copy-start.24 = (bf16[256,512]{1,0:T(8,128)(2,1)}, bf16[256,512]{1,0:T(8,128)(2,1)S(1)}, u32[]{:S(2)}) copy-start(bf16[256,512]{1,0:T(8,128)(2,1)S(1)} %collective-permute-done.9.refs_12_) | copy-start | bytes 786436
  55.9 11.8 %copy-start.25 = (bf16[256,512]{1,0:T(8,128)(2,1)}, bf16[256,512]{1,0:T(8,128)(2,1)S(1)}, u32[]{:S(2)}) copy-start(bf16[256,512]{1,0:T(8,128)(2,1)S(1)} %collective-permute-done.10.refs_13_) | copy-start | bytes 786436
  55.9 9.9 %collective-permute-start.11 = (bf16[256,512]{1,0:T(8,128)(2,1)S(1)}, bf16[256,512]{1,0:T(8,128)(2,1)S(1)}, u32[]{:S(2)}, u32[]{:S(2)}) collective-permute-start(bf16[256,512]{1,0:T(8,128)(2,1)S(1)} %collective-permute-done.7.refs_6_), channel_id=1, source_target_pairs={{0,8},{8,16},{16,24},{24,32},{32,40},{40,48},{48,56},{56,0},{1,9},... | collective-permute-start | bytes 786440 | tf_op jit(solution)/shard_map/ppermute | solution.py:513
  65.8 24.9 %copy-start.26 = (bf16[256,512]{1,0:T(8,128)(2,1)}, bf16[256,512]{1,0:T(8,128)(2,1)S(1)}, u32[]{:S(2)}) copy-start(bf16[256,512]{1,0:T(8,128)(2,1)S(1)} %collective-permute-done.11.refs_8_) | copy-start | bytes 786436
  67.7 4.3 %collective-permute-start.14 = (bf16[8,1024]{1,0:T(8,128)(2,1)S(1)}, bf16[8,1024]{1,0:T(8,128)(2,1)S(1)}, u32[]{:S(2)}, u32[]{:S(2)}) collective-permute-start(bf16[8,1024]{1,0:T(8,128)(2,1)S(1)} %bitcast.12), channel_id=1, source_target_pairs={{0,192},{64,0},{128,64},{192,128},{1,193},{65,1},{129,65},{193,129... | collective-permute-start | bytes 49160 | tf_op jit(solution)/shard_map/ppermute | solution.py:513
  70.3 3.8 %collective-permute-start.13 = (bf16[8,1024]{1,0:T(8,128)(2,1)S(1)}, bf16[8,1024]{1,0:T(8,128)(2,1)S(1)}, u32[]{:S(2)}, u32[]{:S(2)}) collective-permute-start(bf16[8,1024]{1,0:T(8,128)(2,1)S(1)} %bitcast.13), channel_id=1, source_target_pairs={{0,64},{64,128},{128,192},{192,0},{1,65},{65,129},{129,193},{193,1... | collective-permute-start | bytes 49160 | tf_op jit(solution)/shard_map/ppermute | solution.py:513
  70.3 4.1 %collective-permute-start.12 = (bf16[8,1024]{1,0:T(8,128)(2,1)S(1)}, bf16[8,1024]{1,0:T(8,128)(2,1)S(1)}, u32[]{:S(2)}, u32[]{:S(2)}) collective-permute-start(bf16[8,1024]{1,0:T(8,128)(2,1)S(1)} %bitcast.14), channel_id=1, source_target_pairs={{0,128},{64,192},{128,0},{192,64},{1,129},{65,193},{129,1},{193,65... | collective-permute-start | bytes 49160 | tf_op jit(solution)/shard_map/ppermute | solution.py:513
  87.1 5.9 %collective-permute-start.15 = (bf16[256,512]{1,0:T(8,128)(2,1)S(1)}, bf16[256,512]{1,0:T(8,128)(2,1)S(1)}, u32[]{:S(2)}, u32[]{:S(2)}) collective-permute-start(bf16[256,512]{1,0:T(8,128)(2,1)S(1)} %collective-permute-done.7.refs_6_), channel_id=1, source_target_pairs={{0,1},{1,0},{2,3},{3,2},{4,5},{5,4},{6,7},{7,6},{8,9},{9,8},{10,11... | collective-permute-start | bytes 786440 | tf_op jit(solution)/shard_map/ppermute | solution.py:508
  90.5 2.4 %collective-permute-start.16 = (bf16[256,512]{1,0:T(8,128)(2,1)S(1)}, bf16[256,512]{1,0:T(8,128)(2,1)S(1)}, u32[]{:S(2)}, u32[]{:S(2)}) collective-permute-start(bf16[256,512]{1,0:T(8,128)(2,1)S(1)} %collective-permute-done.8.refs_7_), channel_id=1, source_target_pairs={{0,1},{1,0},{2,3},{3,2},{4,5},{5,4},{6,7},{7,6},{8,9},{9,8},{10,11... | collective-permute-start | bytes 786440 | tf_op jit(solution)/shard_map/ppermute | solution.py:508
  90.6 2.4 %collective-permute-start.17 = (bf16[256,512]{1,0:T(8,128)(2,1)S(1)}, bf16[256,512]{1,0:T(8,128)(2,1)S(1)}, u32[]{:S(2)}, u32[]{:S(2)}) collective-permute-start(bf16[256,512]{1,0:T(8,128)(2,1)S(1)} %collective-permute-done.11.refs_8_), channel_id=1, source_target_pairs={{0,1},{1,0},{2,3},{3,2},{4,5},{5,4},{6,7},{7,6},{8,9},{9,8},{10,11... | collective-permute-start | bytes 786440 | tf_op jit(solution)/shard_map/ppermute | solution.py:508
  93.0 11.1 %copy-start.27 = (bf16[256,512]{1,0:T(8,128)(2,1)}, bf16[256,512]{1,0:T(8,128)(2,1)S(1)}, u32[]{:S(2)}) copy-start(bf16[256,512]{1,0:T(8,128)(2,1)S(1)} %collective-permute-done.15.refs_14_) | copy-start | bytes 786436
  104.1 18.8 %all-to-all-start.4 = ((bf16[32,8,1024]{2,1,0:T(8,128)(2,1)}), bf16[32,8,1024]{2,1,0:T(8,128)(2,1)S(1)}, u32[]{:S(2)}, u32[]{:S(2)}) async-start(bf16[32,8,1024]{2,1,0:T(8,128)(2,1)} %get-tuple-element.88), calls=%async_computation.4 | async-start | bytes 1048576 | tf_op jit(solution)/shard_map/all_to_all | solution.py:504
  129.5 20.3 %all-to-all-start.5 = ((f32[64,4,128]{2,1,0:T(4,128)}), f32[64,4,128]{2,1,0:T(4,128)S(1)}, u32[]{:S(2)}, u32[]{:S(2)}) async-start(f32[64,4,128]{2,1,0:T(4,128)} %get-tuple-element.91), calls=%async_computation.5 | async-start | bytes 262144 | tf_op jit(solution)/shard_map/all_to_all | solution.py:504
  138.7 11.1 %copy-start.4 = (bf16[8,8,1152]{2,1,0:T(8,128)(2,1)S(1)}, bf16[8,8,1152]{2,1,0:T(8,128)(2,1)}, u32[]{:S(2)}) copy-start(bf16[8,8,1152]{2,1,0:T(8,128)(2,1)} %copy-done.3) | copy-start | bytes 442372
  138.7 11.1 %copy-start.6 = (f32[8,1024]{1,0:T(8,128)S(1)}, f32[8,1024]{1,0:T(8,128)}, u32[]{:S(2)}) copy-start(f32[8,1024]{1,0:T(8,128)} %copy-done.5) | copy-start | bytes 98308
  138.7 11.1 %copy-start.8 = (s32[11]{0:T(128)S(1)}, s32[11]{0:T(128)}, u32[]{:S(2)}) copy-start(s32[11]{0:T(128)} %pad_add_fusion.refs_0_.pos) | copy-start | bytes 136
  138.7 11.1 %copy-start.11 = (f32[1024,256]{1,0:T(8,128)S(1)}, f32[1024,256]{1,0:T(8,128)}, u32[]{:S(2)}) copy-start(f32[1024,256]{1,0:T(8,128)} %get-tuple-element.96.student_part) | copy-start | bytes 3145732
  160.6 1.7 collective-permute-start.18
  162.5 5.3 %collective-permute-start.21 = (bf16[272,256]{1,0:T(8,128)(2,1)S(1)}, bf16[272,256]{1,0:T(8,128)(2,1)S(1)}, u32[]{:S(2)}, u32[]{:S(2)}) collective-permute-start(bf16[272,256]{1,0:T(8,128)(2,1)S(1)} %get-tuple-element.118), channel_id=1, source_target_pairs={{0,6},{2,0},{4,2},{6,4},{1,7},{3,1},{5,3},{7,5},{8,14},{10,8},{12,... | collective-permute-start | bytes 417800 | tf_op jit(solution)/shard_map/ppermute | solution.py:513
  163.2 6.4 %collective-permute-start.20 = (bf16[272,256]{1,0:T(8,128)(2,1)S(1)}, bf16[272,256]{1,0:T(8,128)(2,1)S(1)}, u32[]{:S(2)}, u32[]{:S(2)}) collective-permute-start(bf16[272,256]{1,0:T(8,128)(2,1)S(1)} %get-tuple-element.118), channel_id=1, source_target_pairs={{0,2},{2,4},{4,6},{6,0},{1,3},{3,5},{5,7},{7,1},{8,10},{10,12},{12... | collective-permute-start | bytes 417800 | tf_op jit(solution)/shard_map/ppermute | solution.py:513
  164.0 7.3 %collective-permute-start.19 = (bf16[272,256]{1,0:T(8,128)(2,1)S(1)}, bf16[272,256]{1,0:T(8,128)(2,1)S(1)}, u32[]{:S(2)}, u32[]{:S(2)}) collective-permute-start(bf16[272,256]{1,0:T(8,128)(2,1)S(1)} %get-tuple-element.118), channel_id=1, source_target_pairs={{0,4},{2,6},{4,0},{6,2},{1,5},{3,7},{5,1},{7,3},{8,12},{10,14},{12... | collective-permute-start | bytes 417800 | tf_op jit(solution)/shard_map/ppermute | solution.py:513
  165.2 8.6 %collective-permute-start.25 = (bf16[256,256]{1,0:T(8,128)(2,1)S(1)}, bf16[256,256]{1,0:T(8,128)(2,1)S(1)}, u32[]{:S(2)}, u32[]{:S(2)}) collective-permute-start(bf16[256,256]{1,0:T(8,128)(2,1)S(1)} %get-tuple-element.106), channel_id=1, source_target_pairs={{0,192},{64,0},{128,64},{192,128},{1,193},{65,1},{129,65},{193,129... | collective-permute-start | bytes 393224 | tf_op jit(solution)/shard_map/ppermute | solution.py:513
  167.2 6.6 %collective-permute-start.24 = (bf16[256,256]{1,0:T(8,128)(2,1)S(1)}, bf16[256,256]{1,0:T(8,128)(2,1)S(1)}, u32[]{:S(2)}, u32[]{:S(2)}) collective-permute-start(bf16[256,256]{1,0:T(8,128)(2,1)S(1)} %get-tuple-element.105), channel_id=1, source_target_pairs={{0,128},{64,192},{128,0},{192,64},{1,129},{65,193},{129,1},{193,65... | collective-permute-start | bytes 393224 | tf_op jit(solution)/shard_map/ppermute | solution.py:513
  167.8 8.4 %collective-permute-start.23 = (bf16[256,256]{1,0:T(8,128)(2,1)S(1)}, bf16[256,256]{1,0:T(8,128)(2,1)S(1)}, u32[]{:S(2)}, u32[]{:S(2)}) collective-permute-start(bf16[256,256]{1,0:T(8,128)(2,1)S(1)} %get-tuple-element.104), channel_id=1, source_target_pairs={{0,64},{64,128},{128,192},{192,0},{1,65},{65,129},{129,193},{193,1... | collective-permute-start | bytes 393224 | tf_op jit(solution)/shard_map/ppermute | solution.py:513
  171.6 5.3 %collective-permute-start.22 = (bf16[272,256]{1,0:T(8,128)(2,1)S(1)}, bf16[272,256]{1,0:T(8,128)(2,1)S(1)}, u32[]{:S(2)}, u32[]{:S(2)}) collective-permute-start(bf16[272,256]{1,0:T(8,128)(2,1)S(1)} %maximum_maximum_fusion.1), channel_id=1, source_target_pairs={{0,1},{1,0},{2,3},{3,2},{4,5},{5,4},{6,7},{7,6},{8,9},{9,8},{10,11... | collective-permute-start | bytes 417800 | tf_op jit(solution)/shard_map/ppermute | solution.py:508
  (12 other events, 67.5 us)
where the time goes:
time: 179 us; the launch traced here: 178 us
  Pallas kernels  61.1 us (34%)
  starting transfers between devices  55.9 us (31%)
  blocking collectives  30.5 us (17%)
  waiting for transfers between devices  15.3 us (9%)
  local copies, waits for them, and re-layouts  11 us (6%)
  other arithmetic  3.32 us (2%)
    all_to_all x3, blocking collectives, gather(): return lax.all_to_all(a, axes, 0, 0)  30.5 us
    ppermute x16, starting transfers between devices, shift(): return lax.ppermute(a, axis, [(i, (i + by) % n) for i in range(n)])  22.4 us
    all_to_all x3, starting transfers between devices, gather(): return lax.all_to_all(a, axes, 0, 0)  21.9 us
    pallas_call x1, Pallas kernels, early(): call(early_kernel, [SCALARS] + [ANY] * (2 * NZ + 3), [ANY, INSIDE, INSIDE...  13.1 us
    ppermute x10, starting transfers between devices, swap_core(): return lax.ppermute(a, 'c', [(0, 1), (1, 0)])  11.6 us
    ppermute x16, waiting for transfers between devices, shift(): return lax.ppermute(a, axis, [(i, (i + by) % n) for i in range(n)])  11.2 us
    pallas_call x1, Pallas kernels, student(): call(student_kernel, [ANY, ANY], [ANY, INSIDE, INSIDE], [shape((NB, BK, D...  10.7 us
    unnamed x62, local copies, waits for them, and re-layouts  9.88 us
  transfers between devices with their start and end apart: 29, of which 9 were waited for; matrix products, arithmetic and copies ran while one was open for 1% of the time, Pallas kernels for 25%

commit v1 on v0

--- a/solution.py
+++ b/solution.py
@@ -71,9 +71,14 @@
 
 
 ANY = pl.BlockSpec(memory_space=pl.ANY)
+OUTSIDE = pl.BlockSpec(memory_space=pltpu.HBM)
 INSIDE = pl.BlockSpec(memory_space=pltpu.VMEM)
 SCALARS = pl.BlockSpec(memory_space=pltpu.SMEM)
 DMA = pltpu.SemaphoreType.DMA
+
+
+def outside(a):
+    return pltpu.with_memory_space_constraint(a, pltpu.HBM)
 
 
 def begin(src, dst, sem):
@@ -229,7 +234,7 @@
 def row_pass(held, got, tot):
     return call(
         row_kernel,
-        [INSIDE, INSIDE, ANY],
+        [INSIDE, INSIDE, OUTSIDE],
         INSIDE,
         shape((NY * NC, 8, 128), f32),
         [pltpu.VMEM((NB, BK), f32), pltpu.VMEM((ROWS, 128), f32), pltpu.VMEM((4, 128), f32), DMA],
@@ -237,7 +242,7 @@
         1 << 16,
         "row_pass",
         SMALL,
-    )(pltpu.with_memory_space_constraint(held, pltpu.VMEM), got, tot)
+    )(pltpu.with_memory_space_constraint(held, pltpu.VMEM), got, outside(tot))
 
 
 def row_last_kernel(expo, got, rows_o, col_o, acc_s):
@@ -410,7 +415,7 @@
 def grad_kernel(
     pos, dirs, rows, stat, got, student_part, col, s_mix, t_mix, cross,
     own_o, next1_o, next2_o, next3_o, keep_o, give_o, line_o,
-    rows_s, got_s, dirs_s, part_s, acc_s, s_mix_s, t_mix_s, small, sems,
+    rows_s, got_s, dirs_s, part_s, acc_s, s_mix_s, t_mix_s, cross_s, small, sems,
 ):
     z, core, x = pos[0], pos[1], pos[2]
     first = [begin(dirs, dirs_s, small.at[1])]
@@ -420,6 +425,7 @@
         begin(got.at[pl.ds(z, 1)], got_s, small.at[2]),
         begin(s_mix, s_mix_s, small.at[3]),
         begin(t_mix, t_mix_s, small.at[4]),
+        begin(cross, cross_s, small.at[0]),
         begin(student_part, part_s, small.at[5]),
     ]
     acc_s[...] = jnp.zeros_like(acc_s)
@@ -457,7 +463,7 @@
     half = ROWS // NC
     keep_o[:half, :] = s_mix_s[pl.ds(pl.multiple_of(core * half, half), half), :]
     give_o[:half, :] = s_mix_s[pl.ds(pl.multiple_of((1 - core) * half, half), half), :].astype(bf16)
-    loss = cross[...] / row_total
+    loss = cross_s[...] / row_total
     low, high = loss[:, :half], loss[:, half:]
     away = jnp.where(core == 0, high, low)
     hi = away.astype(bf16).astype(f32)
@@ -471,7 +477,7 @@
     n, half = NX * DIM, ROWS // NC
     return call(
         grad_kernel,
-        [SCALARS, ANY, ANY, INSIDE, ANY, ANY, INSIDE, ANY, ANY, INSIDE],
+        [SCALARS, ANY, ANY, INSIDE, ANY, ANY, INSIDE, ANY, OUTSIDE, OUTSIDE],
         [INSIDE] * 7,
         [
             shape((DIM, DIM), f32),
@@ -490,6 +496,7 @@
             pltpu.VMEM((n, DIM), f32),
             pltpu.VMEM((ROWS, DIM), f32),
             pltpu.VMEM((ROWS, DIM), f32),
+            pltpu.VMEM((1, ROWS), f32),
             DMA((6,)),
             DMA((NZ,)),
         ],
@@ -497,7 +504,7 @@
         ROWS * COLS,
         "proto_part",
         MIDDLE,
-    )(pos, dirs, rows, stat, got, student_part, col, s_mix, t_mix, cross)
+    )(pos, dirs, rows, stat, got, student_part, col, s_mix, outside(t_mix), outside(cross))
 
 
 def gather(a, axes):

time: 179 us -> 176 us (0.983)
  local copies, waits for them, and re-layouts: 11 us -> 8.59 us
    unnamed x62 -> x54, local copies, waits for them, and re-layouts: 9.88 us -> 7.48 us
  transfers between devices with their start and end apart: 29 -> 29, of which waited for: 9 -> 9; matrix products, arithmetic and copies ran while one was open for 1% -> 1% of each run, Pallas kernels for 25% -> 26%
where the time goes in v1:
time: 176 us
  Pallas kernels  61.1 us (35%)
  starting transfers between devices  55.7 us (32%)
  blocking collectives  30.6 us (17%)
  waiting for transfers between devices  15.3 us (9%)
  local copies, waits for them, and re-layouts  8.59 us (5%)
  other arithmetic  3.33 us (2%)
    all_to_all x3, blocking collectives, gather(): return lax.all_to_all(a, axes, 0, 0)  30.6 us
    ppermute x16, starting transfers between devices, shift(): return lax.ppermute(a, axis, [(i, (i + by) % n) for i in range(n)])  22.2 us
    all_to_all x3, starting transfers between devices, gather(): return lax.all_to_all(a, axes, 0, 0)  21.9 us
    pallas_call x1, Pallas kernels, early(): call(early_kernel, [SCALARS] + [ANY] * (2 * NZ + 3), [ANY, INSIDE, INSIDE...  13.1 us
    ppermute x10, starting transfers between devices, swap_core(): return lax.ppermute(a, 'c', [(0, 1), (1, 0)])  11.6 us
    ppermute x16, waiting for transfers between devices, shift(): return lax.ppermute(a, axis, [(i, (i + by) % n) for i in range(n)])  11.2 us
    pallas_call x1, Pallas kernels, student(): call(student_kernel, [ANY, ANY], [ANY, INSIDE, INSIDE], [shape((NB, BK, D...  10.7 us
    pallas_call x1, Pallas kernels, proto_part(): call(grad_kernel, [SCALARS, ANY, ANY, INSIDE, ANY, ANY, INSIDE, ANY, OUTS...  8.98 us
  transfers between devices with their start and end apart: 29, of which 9 were waited for; matrix products, arithmetic and copies ran while one was open for 1% of the time, Pallas kernels for 26%

profile of v1, /device:TPU:1, one launch (start us, length us, event | category | flops | bytes accessed | tf_op | source)
XLA Modules:
  0.0 175.8 jit_solution(9554138204409682651)
XLA Ops:
  0.6 1.0 constant_dynamic-slice_fusion
  1.7 2.5 %collective-permute-start = (bf16[256,512]{1,0:T(8,128)(2,1)S(1)}, bf16[256,512]{1,0:T(8,128)(2,1)S(1)}, u32[]{:S(2)}, u32[]{:S(2)}) collective-permute-start(bf16[256,512]{1,0:T(8,128)(2,1)S(1)} %pad_maximum_fusion.refs_1_), channel_id=1, source_target_pairs={{0,8},{8,16},{16,24},{24,32},{32,40},{40,48},{48,56},{56,0},{1,9},... | collective-permute-start | bytes 786440 | tf_op jit(solution)/shard_map/ppermute | solution.py:520
  4.2 4.0 %collective-permute-start.1 = (bf16[256,512]{1,0:T(8,128)(2,1)S(1)}, bf16[256,512]{1,0:T(8,128)(2,1)S(1)}, u32[]{:S(2)}, u32[]{:S(2)}) collective-permute-start(bf16[256,512]{1,0:T(8,128)(2,1)S(1)} %pad_maximum_fusion.refs_1_), channel_id=1, source_target_pairs={{0,56},{8,0},{16,8},{24,16},{32,24},{40,32},{48,40},{56,48},{1,57}... | collective-permute-start | bytes 786440 | tf_op jit(solution)/shard_map/ppermute | solution.py:520
  8.2 8.9 %teacher.1 = (bf16[8,512,1024]{2,1,0:T(8,128)(2,1)}, bf16[32,8,1024]{2,1,0:T(8,128)(2,1)}) custom-call(bf16[512,256]{1,0:T(8,128)(2,1)} %feat.3, bf16[8,1024,256]{2,1,0:T(8,128)(2,1)} %bitcast.18), custom_call_target="tpu_custom_call" | custom-call | flops 2147483648 | bytes 12582912 | tf_op jit(solution)/shard_map/teacher/pallas_call | solution.py:127
  17.2 8.1 %all-to-all-start = ((bf16[32,8,1024]{2,1,0:T(8,128)(2,1)}), bf16[32,8,1024]{2,1,0:T(8,128)(2,1)S(1)}, u32[]{:S(2)}, u32[]{:S(2)}) async-start(bf16[32,8,1024]{2,1,0:T(8,128)(2,1)} %get-tuple-element.58), calls=%async_computation | async-start | bytes 1048576 | tf_op jit(solution)/shard_map/all_to_all | solution.py:511
  25.3 1.6 collective-permute-start.4
  26.9 1.5 collective-permute-start.2
  28.8 1.2 collective-permute-start.3
  30.4 10.7 %student.1 = (bf16[8,1024,256]{2,1,0:T(8,128)(2,1)}, f32[4,128]{1,0:T(4,128)}, f32[512,256]{1,0:T(8,128)}) custom-call(bf16[512,256]{1,0:T(8,128)(2,1)} %feat.5, bf16[8,1024,256]{2,1,0:T(8,128)(2,1)} %bitcast.17), custom_call_target="tpu_custom_call" | custom-call | flops 4294967296 | bytes 8388608 | tf_op jit(solution)/shard_map/student/pallas_call | solution.py:179
  41.1 3.5 %collective-permute-done.2.refs_4_ = bf16[256,512]{1,0:T(8,128)(2,1)S(1)} collective-permute-done((bf16[256,512]{1,0:T(8,128)(2,1)S(1)}, bf16[256,512]{1,0:T(8,128)(2,1)S(1)}, u32[]{:S(2)}, u32[]{:S(2)}) %collective-permute-start.2) | collective-permute-done | bytes 262176 | tf_op jit(solution)/shard_map/ppermute | solution.py:520
  44.9 2.5 %collective-permute-start.8 = (bf16[256,512]{1,0:T(8,128)(2,1)S(1)}, bf16[256,512]{1,0:T(8,128)(2,1)S(1)}, u32[]{:S(2)}, u32[]{:S(2)}) collective-permute-start(bf16[256,512]{1,0:T(8,128)(2,1)S(1)} %collective-permute-done.3.refs_5_), channel_id=1, source_target_pairs={{0,56},{8,0},{16,8},{24,16},{32,24},{40,32},{48,40},{56,48},{1,57}... | collective-permute-start | bytes 786440 | tf_op jit(solution)/shard_map/ppermute | solution.py:520
  47.4 2.3 %collective-permute-start.9 = (bf16[256,512]{1,0:T(8,128)(2,1)S(1)}, bf16[256,512]{1,0:T(8,128)(2,1)S(1)}, u32[]{:S(2)}, u32[]{:S(2)}) collective-permute-start(bf16[256,512]{1,0:T(8,128)(2,1)S(1)} %collective-permute-done.2.refs_4_), channel_id=1, source_target_pairs={{0,1},{1,0},{2,3},{3,2},{4,5},{5,4},{6,7},{7,6},{8,9},{9,8},{10,11... | collective-permute-start | bytes 786440 | tf_op jit(solution)/shard_map/ppermute | solution.py:515
  49.7 3.4 %copy-done = bf16[8,512,1024]{2,1,0:T(8,128)(2,1)S(1)} copy-done((bf16[8,512,1024]{2,1,0:T(8,128)(2,1)S(1)}, bf16[8,512,1024]{2,1,0:T(8,128)(2,1)}, u32[]{:S(2)}) %copy-start) | copy-done | bytes 8388632
  53.1 1.9 %row_pass.2 = f32[8,8,128]{2,1,0:T(8,128)S(1)} custom-call(bf16[8,512,1024]{2,1,0:T(8,128)(2,1)S(1)} %copy-done, bf16[32,8,1024]{2,1,0:T(8,128)(2,1)S(1)} %all-to-all-done.got, f32[4,128]{1,0:T(4,128)} %get-tuple-element.64.tot), custom_call_target="tpu_custom_call" | custom-call | flops 8388608 | bytes 65536 | tf_op jit(solution)/shard_map/row_pass/pallas_call | solution.py:235
  55.2 10.2 %all_to_all.30.got = f32[8,8,128]{2,1,0:T(8,128)S(1)} all-to-all(f32[8,8,128]{2,1,0:T(8,128)S(1)} %row_pass.2), channel_id=1, replica_groups=mesh['x'=4,'z'=8,'y'=4,'c'=2] {'y','c'}, dimensions={0} | all-to-all | bytes 65536 | tf_op jit(solution)/shard_map/all_to_all | solution.py:511
  65.5 1.9 %col_pass.2 = (bf16[1,8,1024]{2,1,0:T(8,128)(2,1)S(1)}, bf16[8,128]{1,0:T(8,128)(2,1)S(1)}) custom-call(bf16[8,512,1024]{2,1,0:T(8,128)(2,1)S(1)} %copy-done, f32[8,8,128]{2,1,0:T(8,128)S(1)} %all_to_all.30.got), custom_call_target="tpu_custom_call" | custom-call | flops 8388608 | bytes 1048576 | tf_op jit(solution)/shard_map/col_pass/pallas_call | solution.py:289
  67.4 2.5 %collective-permute-start.14 = (bf16[8,1024]{1,0:T(8,128)(2,1)S(1)}, bf16[8,1024]{1,0:T(8,128)(2,1)S(1)}, u32[]{:S(2)}, u32[]{:S(2)}) collective-permute-start(bf16[8,1024]{1,0:T(8,128)(2,1)S(1)} %bitcast.12), channel_id=1, source_target_pairs={{0,192},{64,0},{128,64},{192,128},{1,193},{65,1},{129,65},{193,129... | collective-permute-start | bytes 49160 | tf_op jit(solution)/shard_map/ppermute | solution.py:520
  69.9 1.7 collective-permute-start.12
  71.6 2.1 %collective-permute-done.13 = bf16[8,1024]{1,0:T(8,128)(2,1)S(1)} collective-permute-done((bf16[8,1024]{1,0:T(8,128)(2,1)S(1)}, bf16[8,1024]{1,0:T(8,128)(2,1)S(1)}, u32[]{:S(2)}, u32[]{:S(2)}) %collective-permute-start.13) | collective-permute-done | bytes 16416 | tf_op jit(solution)/shard_map/ppermute | solution.py:520
  74.1 12.3 %all_to_all.31.got.refs_19_ = bf16[8,8,1152]{2,1,0:T(8,128)(2,1)S(1)} all-to-all(bf16[8,8,1152]{2,1,0:T(8,128)(2,1)S(1)} %broadcast_in_dim.2), channel_id=1, replica_groups=mesh['x'=4,'z'=8,'y'=4,'c'=2] {'z'}, dimensions={0} | all-to-all | bytes 294912 | tf_op jit(solution)/shard_map/all_to_all | solution.py:511
  86.4 3.5 %collective-permute-start.15 = (bf16[256,512]{1,0:T(8,128)(2,1)S(1)}, bf16[256,512]{1,0:T(8,128)(2,1)S(1)}, u32[]{:S(2)}, u32[]{:S(2)}) collective-permute-start(bf16[256,512]{1,0:T(8,128)(2,1)S(1)} %collective-permute-done.7.refs_6_), channel_id=1, source_target_pairs={{0,1},{1,0},{2,3},{3,2},{4,5},{5,4},{6,7},{7,6},{8,9},{9,8},{10,11... | collective-permute-start | bytes 786440 | tf_op jit(solution)/shard_map/ppermute | solution.py:515
  90.4 1.9 %row_pass.3 = f32[8,8,128]{2,1,0:T(8,128)S(1)} custom-call(bf16[8,512,1024]{2,1,0:T(8,128)(2,1)S(1)} %copy-done, bf16[8,8,1152]{2,1,0:T(8,128)(2,1)S(1)} %all_to_all.31.got.refs_19_, f32[4,128]{1,0:T(4,128)} %get-tuple-element.64.tot), custom_call_target="tpu_custom_call" | custom-call | flops 8388608 | bytes 65536 | tf_op jit(solution)/shard_map/row_pass/pallas_call | solution.py:235
  92.3 8.0 %all_to_all.32.got = f32[8,8,128]{2,1,0:T(8,128)S(1)} all-to-all(f32[8,8,128]{2,1,0:T(8,128)S(1)} %row_pass.3), channel_id=1, replica_groups=mesh['x'=4,'z'=8,'y'=4,'c'=2] {'y','c'}, dimensions={0} | all-to-all | bytes 65536 | tf_op jit(solution)/shard_map/all_to_all | solution.py:511
  100.4 2.7 %col_pass.3 = (bf16[32,8,1024]{2,1,0:T(8,128)(2,1)}, bf16[8,128]{1,0:T(8,128)(2,1)}) custom-call(bf16[8,512,1024]{2,1,0:T(8,128)(2,1)S(1)} %copy-done, f32[8,8,128]{2,1,0:T(8,128)S(1)} %all_to_all.32.got), custom_call_target="tpu_custom_call" | custom-call | flops 8388608 | bytes 1048576 | tf_op jit(solution)/shard_map/col_pass/pallas_call | solution.py:289
  103.1 4.6 %all-to-all-start.4 = ((bf16[32,8,1024]{2,1,0:T(8,128)(2,1)}), bf16[32,8,1024]{2,1,0:T(8,128)(2,1)S(1)}, u32[]{:S(2)}, u32[]{:S(2)}) async-start(bf16[32,8,1024]{2,1,0:T(8,128)(2,1)} %get-tuple-element.88), calls=%async_computation.4 | async-start | bytes 1048576 | tf_op jit(solution)/shard_map/all_to_all | solution.py:511
  107.8 0.7 pad_add_fusion.refs_0_.pos
  108.5 13.1 %early.1 = (bf16[8,512,512]{2,1,0:T(8,128)(2,1)}, bf16[1024,256]{1,0:T(8,128)(2,1)}, f32[1024,256]{1,0:T(8,128)}) custom-call(s32[11]{0:T(128)} %pad_add_fusion.refs_0_.pos, bf16[256,512]{1,0:T(8,128)(2,1)} %copy-done.10, bf16[256,512]{1,0:T(8,128)(2,1)} %copy-done.11, bf16[256,512]{1,0:T(8,128)(2,1)} %copy-done.12, bf16[256,512]{1,0:T(8,128)(2,1)} %copy-done.14, ...), custom_call_target="tpu_custom_call" | custom-call | flops 4294967296 | bytes 4194304 | tf_op jit(solution)/shard_map/early/pallas_call | solution.py:385
  122.0 3.4 %copy-done.1 = bf16[8,512,1024]{2,1,0:T(8,128)(2,1)S(1)} copy-done((bf16[8,512,1024]{2,1,0:T(8,128)(2,1)S(1)}, bf16[8,512,1024]{2,1,0:T(8,128)(2,1)}, u32[]{:S(2)}) %copy-start.1) | copy-done | bytes 8388632
  125.4 2.6 %row_last.1 = (f32[64,4,128]{2,1,0:T(4,128)}, f32[8,1024]{1,0:T(8,128)S(1)}) custom-call(bf16[8,512,1024]{2,1,0:T(8,128)(2,1)S(1)} %copy-done.1, bf16[32,8,1024]{2,1,0:T(8,128)(2,1)S(1)} %all-to-all-done.4.got), custom_call_target="tpu_custom_call" | custom-call | flops 8388608 | bytes 65536 | tf_op jit(solution)/shard_map/row_last/pallas_call | solution.py:254
  128.0 0.6 copy-done.4
  128.6 9.2 %all-to-all-start.5 = ((f32[64,4,128]{2,1,0:T(4,128)}), f32[64,4,128]{2,1,0:T(4,128)S(1)}, u32[]{:S(2)}, u32[]{:S(2)}) async-start(f32[64,4,128]{2,1,0:T(4,128)} %get-tuple-element.91), calls=%async_computation.5 | async-start | bytes 262144 | tf_op jit(solution)/shard_map/all_to_all | solution.py:511
  137.8 8.3 %mix_pass.1 = (f32[512,256]{1,0:T(8,128)}, f32[1,512]{1,0:T(1,128)}) custom-call(bf16[8,512,1024]{2,1,0:T(8,128)(2,1)} %get-tuple-element.62.expo, f32[8,1024]{1,0:T(8,128)} %copy-done.4, bf16[8,1024,256]{2,1,0:T(8,128)(2,1)} %get-tuple-element.84.dirs, bf16[512,256]{1,0:T(8,128)(2,1)} %feat.5), custom_call_target="tpu_custom_call" | custom-call | flops 2147483648 | bytes 12582912 | tf_op jit(solution)/shard_map/mix_pass/pallas_call | solution.py:327
  146.1 2.7 %all-to-all-done.5 = f32[64,4,128]{2,1,0:T(4,128)S(1)} async-done(((f32[64,4,128]{2,1,0:T(4,128)}), f32[64,4,128]{2,1,0:T(4,128)S(1)}, u32[]{:S(2)}, u32[]{:S(2)}) %all-to-all-start.5) | async-done | bytes 131104 | tf_op jit(solution)/shard_map/all_to_all | solution.py:511
  148.9 9.0 %proto_part.1 = (f32[256,256]{1,0:T(8,128)S(1)}, bf16[256,256]{1,0:T(8,128)(2,1)S(1)}, bf16[256,256]{1,0:T(8,128)(2,1)S(1)}, bf16[256,256]{1,0:T(8,128)(2,1)S(1)...) custom-call(s32[11]{0:T(128)S(1)} %copy-done.6, bf16[1024,256]{1,0:T(8,128)(2,1)S(1)} %copy-done.8, ...), custom_call_target="tpu_custom_call" | custom-call | flops 4294967296 | bytes 4194304 | tf_op jit(solution)/shard_map/proto_part/pallas_call | solution.py:478
  157.9 0.7 collective-permute-start.18
  158.7 0.9 collective-permute-done.18
  159.8 0.7 collective-permute-start.21
  160.5 0.9 collective-permute-start.20
  161.4 1.2 collective-permute-start.19
  162.6 2.1 %collective-permute-start.25 = (bf16[256,256]{1,0:T(8,128)(2,1)S(1)}, bf16[256,256]{1,0:T(8,128)(2,1)S(1)}, u32[]{:S(2)}, u32[]{:S(2)}) collective-permute-start(bf16[256,256]{1,0:T(8,128)(2,1)S(1)} %get-tuple-element.106), channel_id=1, source_target_pairs={{0,192},{64,0},{128,64},{192,128},{1,193},{65,1},{129,65},{193,129... | collective-permute-start | bytes 393224 | tf_op jit(solution)/shard_map/ppermute | solution.py:520
  165.1 0.6 collective-permute-start.23
  165.7 1.1 collective-permute-done.20
  166.9 1.8 %collective-permute-done.19 = bf16[272,256]{1,0:T(8,128)(2,1)S(1)} collective-permute-done((bf16[272,256]{1,0:T(8,128)(2,1)S(1)}, bf16[272,256]{1,0:T(8,128)(2,1)S(1)}, u32[]{:S(2)}, u32[]{:S(2)}) %collective-permute-start.19) | collective-permute-done | bytes 139296 | tf_op jit(solution)/shard_map/ppermute | solution.py:520
  168.9 2.2 %collective-permute-start.22 = (bf16[272,256]{1,0:T(8,128)(2,1)S(1)}, bf16[272,256]{1,0:T(8,128)(2,1)S(1)}, u32[]{:S(2)}, u32[]{:S(2)}) collective-permute-start(bf16[272,256]{1,0:T(8,128)(2,1)S(1)} %maximum_maximum_fusion.1), channel_id=1, source_target_pairs={{0,1},{1,0},{2,3},{3,2},{4,5},{5,4},{6,7},{7,6},{8,9},{9,8},{10,11... | collective-permute-start | bytes 417800 | tf_op jit(solution)/shard_map/ppermute | solution.py:515
  171.2 2.4 %collective-permute-done.23 = bf16[256,256]{1,0:T(8,128)(2,1)S(1)} collective-permute-done((bf16[256,256]{1,0:T(8,128)(2,1)S(1)}, bf16[256,256]{1,0:T(8,128)(2,1)S(1)}, u32[]{:S(2)}, u32[]{:S(2)}) %collective-permute-start.23) | collective-permute-done | bytes 131104 | tf_op jit(solution)/shard_map/ppermute | solution.py:520
  173.6 0.7 add_convert_fusion
  174.5 0.7 pad_maximum_fusion.1
  175.2 0.6 maximum_subtract_fusion
  (106 shorter events, 3.8 us)
Async XLA Ops:
  1.7 23.6 %copy-start.10 = (bf16[256,512]{1,0:T(8,128)(2,1)}, bf16[256,512]{1,0:T(8,128)(2,1)S(1)}, u32[]{:S(2)}) copy-start(bf16[256,512]{1,0:T(8,128)(2,1)S(1)} %pad_maximum_fusion.refs_1_) | copy-start | bytes 786436
  1.7 15.5 %collective-permute-start = (bf16[256,512]{1,0:T(8,128)(2,1)S(1)}, bf16[256,512]{1,0:T(8,128)(2,1)S(1)}, u32[]{:S(2)}, u32[]{:S(2)}) collective-permute-start(bf16[256,512]{1,0:T(8,128)(2,1)S(1)} %pad_maximum_fusion.refs_1_), channel_id=1, source_target_pairs={{0,8},{8,16},{16,24},{24,32},{32,40},{40,48},{48,56},{56,0},{1,9},... | collective-permute-start | bytes 786440 | tf_op jit(solution)/shard_map/ppermute | solution.py:520
  4.2 13.0 %collective-permute-start.1 = (bf16[256,512]{1,0:T(8,128)(2,1)S(1)}, bf16[256,512]{1,0:T(8,128)(2,1)S(1)}, u32[]{:S(2)}, u32[]{:S(2)}) collective-permute-start(bf16[256,512]{1,0:T(8,128)(2,1)S(1)} %pad_maximum_fusion.refs_1_), channel_id=1, source_target_pairs={{0,56},{8,0},{16,8},{24,16},{32,24},{40,32},{48,40},{56,48},{1,57}... | collective-permute-start | bytes 786440 | tf_op jit(solution)/shard_map/ppermute | solution.py:520
  17.2 23.9 %copy-start.11 = (bf16[256,512]{1,0:T(8,128)(2,1)}, bf16[256,512]{1,0:T(8,128)(2,1)S(1)}, u32[]{:S(2)}) copy-start(bf16[256,512]{1,0:T(8,128)(2,1)S(1)} %collective-permute-done.refs_2_) | copy-start | bytes 786436
  17.2 23.9 %copy-start.12 = (bf16[256,512]{1,0:T(8,128)(2,1)}, bf16[256,512]{1,0:T(8,128)(2,1)S(1)}, u32[]{:S(2)}) copy-start(bf16[256,512]{1,0:T(8,128)(2,1)S(1)} %collective-permute-done.1.refs_3_) | copy-start | bytes 786436
  17.2 27.4 %all-to-all-start = ((bf16[32,8,1024]{2,1,0:T(8,128)(2,1)}), bf16[32,8,1024]{2,1,0:T(8,128)(2,1)S(1)}, u32[]{:S(2)}, u32[]{:S(2)}) async-start(bf16[32,8,1024]{2,1,0:T(8,128)(2,1)} %get-tuple-element.58), calls=%async_computation | async-start | bytes 1048576 | tf_op jit(solution)/shard_map/all_to_all | solution.py:511
  25.3 15.8 %collective-permute-start.4 = (bf16[256,512]{1,0:T(8,128)(2,1)S(1)}, bf16[256,512]{1,0:T(8,128)(2,1)S(1)}, u32[]{:S(2)}, u32[]{:S(2)}) collective-permute-start(bf16[256,512]{1,0:T(8,128)(2,1)S(1)} %pad_maximum_fusion.refs_1_), channel_id=1, source_target_pairs={{0,1},{1,0},{2,3},{3,2},{4,5},{5,4},{6,7},{7,6},{8,9},{9,8},{10,11... | collective-permute-start | bytes 786440 | tf_op jit(solution)/shard_map/ppermute | solution.py:515
  26.9 17.7 %collective-permute-start.2 = (bf16[256,512]{1,0:T(8,128)(2,1)S(1)}, bf16[256,512]{1,0:T(8,128)(2,1)S(1)}, u32[]{:S(2)}, u32[]{:S(2)}) collective-permute-start(bf16[256,512]{1,0:T(8,128)(2,1)S(1)} %collective-permute-done.refs_2_), channel_id=1, source_target_pairs={{0,8},{8,16},{16,24},{24,32},{32,40},{40,48},{48,56},{56,0},{1,9},... | collective-permute-start | bytes 786440 | tf_op jit(solution)/shard_map/ppermute | solution.py:520
  28.4 16.2 %collective-permute-start.5 = (bf16[256,512]{1,0:T(8,128)(2,1)S(1)}, bf16[256,512]{1,0:T(8,128)(2,1)S(1)}, u32[]{:S(2)}, u32[]{:S(2)}) collective-permute-start(bf16[256,512]{1,0:T(8,128)(2,1)S(1)} %collective-permute-done.refs_2_), channel_id=1, source_target_pairs={{0,1},{1,0},{2,3},{3,2},{4,5},{5,4},{6,7},{7,6},{8,9},{9,8},{10,11... | collective-permute-start | bytes 786440 | tf_op jit(solution)/shard_map/ppermute | solution.py:515
  28.8 15.8 %collective-permute-start.3 = (bf16[256,512]{1,0:T(8,128)(2,1)S(1)}, bf16[256,512]{1,0:T(8,128)(2,1)S(1)}, u32[]{:S(2)}, u32[]{:S(2)}) collective-permute-start(bf16[256,512]{1,0:T(8,128)(2,1)S(1)} %collective-permute-done.1.refs_3_), channel_id=1, source_target_pairs={{0,56},{8,0},{16,8},{24,16},{32,24},{40,32},{48,40},{56,48},{1,57}... | collective-permute-start | bytes 786440 | tf_op jit(solution)/shard_map/ppermute | solution.py:520
  29.9 14.7 %collective-permute-start.6 = (bf16[256,512]{1,0:T(8,128)(2,1)S(1)}, bf16[256,512]{1,0:T(8,128)(2,1)S(1)}, u32[]{:S(2)}, u32[]{:S(2)}) collective-permute-start(bf16[256,512]{1,0:T(8,128)(2,1)S(1)} %collective-permute-done.1.refs_3_), channel_id=1, source_target_pairs={{0,1},{1,0},{2,3},{3,2},{4,5},{5,4},{6,7},{7,6},{8,9},{9,8},{10,11... | collective-permute-start | bytes 786440 | tf_op jit(solution)/shard_map/ppermute | solution.py:515
  41.1 13.9 %copy-start.13 = (bf16[256,512]{1,0:T(8,128)(2,1)}, bf16[256,512]{1,0:T(8,128)(2,1)S(1)}, u32[]{:S(2)}) copy-start(bf16[256,512]{1,0:T(8,128)(2,1)S(1)} %collective-permute-done.4.refs_9_) | copy-start | bytes 786436
  44.6 10.4 %copy-start.15 = (bf16[256,512]{1,0:T(8,128)(2,1)}, bf16[256,512]{1,0:T(8,128)(2,1)S(1)}, u32[]{:S(2)}) copy-start(bf16[256,512]{1,0:T(8,128)(2,1)S(1)} %collective-permute-done.5.refs_10_) | copy-start | bytes 786436
  44.7 10.4 %collective-permute-start.7 = (bf16[256,512]{1,0:T(8,128)(2,1)S(1)}, bf16[256,512]{1,0:T(8,128)(2,1)S(1)}, u32[]{:S(2)}, u32[]{:S(2)}) collective-permute-start(bf16[256,512]{1,0:T(8,128)(2,1)S(1)} %collective-permute-done.2.refs_4_), channel_id=1, source_target_pairs={{0,8},{8,16},{16,24},{24,32},{32,40},{40,48},{48,56},{56,0},{1,9},... | collective-permute-start | bytes 786440 | tf_op jit(solution)/shard_map/ppermute | solution.py:520
  44.9 10.2 %collective-permute-start.8 = (bf16[256,512]{1,0:T(8,128)(2,1)S(1)}, bf16[256,512]{1,0:T(8,128)(2,1)S(1)}, u32[]{:S(2)}, u32[]{:S(2)}) collective-permute-start(bf16[256,512]{1,0:T(8,128)(2,1)S(1)} %collective-permute-done.3.refs_5_), channel_id=1, source_target_pairs={{0,56},{8,0},{16,8},{24,16},{32,24},{40,32},{48,40},{56,48},{1,57}... | collective-permute-start | bytes 786440 | tf_op jit(solution)/shard_map/ppermute | solution.py:520
  47.4 7.7 %collective-permute-start.9 = (bf16[256,512]{1,0:T(8,128)(2,1)S(1)}, bf16[256,512]{1,0:T(8,128)(2,1)S(1)}, u32[]{:S(2)}, u32[]{:S(2)}) collective-permute-start(bf16[256,512]{1,0:T(8,128)(2,1)S(1)} %collective-permute-done.2.refs_4_), channel_id=1, source_target_pairs={{0,1},{1,0},{2,3},{3,2},{4,5},{5,4},{6,7},{7,6},{8,9},{9,8},{10,11... | collective-permute-start | bytes 786440 | tf_op jit(solution)/shard_map/ppermute | solution.py:515
  49.7 5.4 %collective-permute-start.10 = (bf16[256,512]{1,0:T(8,128)(2,1)S(1)}, bf16[256,512]{1,0:T(8,128)(2,1)S(1)}, u32[]{:S(2)}, u32[]{:S(2)}) collective-permute-start(bf16[256,512]{1,0:T(8,128)(2,1)S(1)} %collective-permute-done.3.refs_5_), channel_id=1, source_target_pairs={{0,1},{1,0},{2,3},{3,2},{4,5},{5,4},{6,7},{7,6},{8,9},{9,8},{10,11... | collective-permute-start | bytes 786440 | tf_op jit(solution)/shard_map/ppermute | solution.py:515
  55.1 31.3 %copy-start.18 = (bf16[256,512]{1,0:T(8,128)(2,1)}, bf16[256,512]{1,0:T(8,128)(2,1)S(1)}, u32[]{:S(2)}) copy-start(bf16[256,512]{1,0:T(8,128)(2,1)S(1)} %collective-permute-done.7.refs_6_) | copy-start | bytes 786436
  55.1 34.8 %copy-start.19 = (bf16[256,512]{1,0:T(8,128)(2,1)}, bf16[256,512]{1,0:T(8,128)(2,1)S(1)}, u32[]{:S(2)}) copy-start(bf16[256,512]{1,0:T(8,128)(2,1)S(1)} %collective-permute-done.8.refs_7_) | copy-start | bytes 786436
  55.1 12.3 %copy-start.20 = (bf16[256,512]{1,0:T(8,128)(2,1)}, bf16[256,512]{1,0:T(8,128)(2,1)S(1)}, u32[]{:S(2)}) copy-start(bf16[256,512]{1,0:T(8,128)(2,1)S(1)} %collective-permute-done.9.refs_12_) | copy-start | bytes 786436
  55.1 12.2 %copy-start.21 = (bf16[256,512]{1,0:T(8,128)(2,1)}, bf16[256,512]{1,0:T(8,128)(2,1)S(1)}, u32[]{:S(2)}) copy-start(bf16[256,512]{1,0:T(8,128)(2,1)S(1)} %collective-permute-done.10.refs_13_) | copy-start | bytes 786436
  55.2 10.3 %collective-permute-start.11 = (bf16[256,512]{1,0:T(8,128)(2,1)S(1)}, bf16[256,512]{1,0:T(8,128)(2,1)S(1)}, u32[]{:S(2)}, u32[]{:S(2)}) collective-permute-start(bf16[256,512]{1,0:T(8,128)(2,1)S(1)} %collective-permute-done.7.refs_6_), channel_id=1, source_target_pairs={{0,8},{8,16},{16,24},{24,32},{32,40},{40,48},{48,56},{56,0},{1,9},... | collective-permute-start | bytes 786440 | tf_op jit(solution)/shard_map/ppermute | solution.py:520
  65.5 24.5 %copy-start.22 = (bf16[256,512]{1,0:T(8,128)(2,1)}, bf16[256,512]{1,0:T(8,128)(2,1)S(1)}, u32[]{:S(2)}) copy-start(bf16[256,512]{1,0:T(8,128)(2,1)S(1)} %collective-permute-done.11.refs_8_) | copy-start | bytes 786436
  67.4 4.2 %collective-permute-start.14 = (bf16[8,1024]{1,0:T(8,128)(2,1)S(1)}, bf16[8,1024]{1,0:T(8,128)(2,1)S(1)}, u32[]{:S(2)}, u32[]{:S(2)}) collective-permute-start(bf16[8,1024]{1,0:T(8,128)(2,1)S(1)} %bitcast.12), channel_id=1, source_target_pairs={{0,192},{64,0},{128,64},{192,128},{1,193},{65,1},{129,65},{193,129... | collective-permute-start | bytes 49160 | tf_op jit(solution)/shard_map/ppermute | solution.py:520
  69.9 3.8 %collective-permute-start.13 = (bf16[8,1024]{1,0:T(8,128)(2,1)S(1)}, bf16[8,1024]{1,0:T(8,128)(2,1)S(1)}, u32[]{:S(2)}, u32[]{:S(2)}) collective-permute-start(bf16[8,1024]{1,0:T(8,128)(2,1)S(1)} %bitcast.13), channel_id=1, source_target_pairs={{0,64},{64,128},{128,192},{192,0},{1,65},{65,129},{129,193},{193,1... | collective-permute-start | bytes 49160 | tf_op jit(solution)/shard_map/ppermute | solution.py:520
  69.9 4.1 %collective-permute-start.12 = (bf16[8,1024]{1,0:T(8,128)(2,1)S(1)}, bf16[8,1024]{1,0:T(8,128)(2,1)S(1)}, u32[]{:S(2)}, u32[]{:S(2)}) collective-permute-start(bf16[8,1024]{1,0:T(8,128)(2,1)S(1)} %bitcast.14), channel_id=1, source_target_pairs={{0,128},{64,192},{128,0},{192,64},{1,129},{65,193},{129,1},{193,65... | collective-permute-start | bytes 49160 | tf_op jit(solution)/shard_map/ppermute | solution.py:520
  86.4 5.9 %collective-permute-start.15 = (bf16[256,512]{1,0:T(8,128)(2,1)S(1)}, bf16[256,512]{1,0:T(8,128)(2,1)S(1)}, u32[]{:S(2)}, u32[]{:S(2)}) collective-permute-start(bf16[256,512]{1,0:T(8,128)(2,1)S(1)} %collective-permute-done.7.refs_6_), channel_id=1, source_target_pairs={{0,1},{1,0},{2,3},{3,2},{4,5},{5,4},{6,7},{7,6},{8,9},{9,8},{10,11... | collective-permute-start | bytes 786440 | tf_op jit(solution)/shard_map/ppermute | solution.py:515
  89.9 2.4 %collective-permute-start.16 = (bf16[256,512]{1,0:T(8,128)(2,1)S(1)}, bf16[256,512]{1,0:T(8,128)(2,1)S(1)}, u32[]{:S(2)}, u32[]{:S(2)}) collective-permute-start(bf16[256,512]{1,0:T(8,128)(2,1)S(1)} %collective-permute-done.8.refs_7_), channel_id=1, source_target_pairs={{0,1},{1,0},{2,3},{3,2},{4,5},{5,4},{6,7},{7,6},{8,9},{9,8},{10,11... | collective-permute-start | bytes 786440 | tf_op jit(solution)/shard_map/ppermute | solution.py:515
  90.0 2.3 %collective-permute-start.17 = (bf16[256,512]{1,0:T(8,128)(2,1)S(1)}, bf16[256,512]{1,0:T(8,128)(2,1)S(1)}, u32[]{:S(2)}, u32[]{:S(2)}) collective-permute-start(bf16[256,512]{1,0:T(8,128)(2,1)S(1)} %collective-permute-done.11.refs_8_), channel_id=1, source_target_pairs={{0,1},{1,0},{2,3},{3,2},{4,5},{5,4},{6,7},{7,6},{8,9},{9,8},{10,11... | collective-permute-start | bytes 786440 | tf_op jit(solution)/shard_map/ppermute | solution.py:515
  92.3 10.8 %copy-start.23 = (bf16[256,512]{1,0:T(8,128)(2,1)}, bf16[256,512]{1,0:T(8,128)(2,1)S(1)}, u32[]{:S(2)}) copy-start(bf16[256,512]{1,0:T(8,128)(2,1)S(1)} %collective-permute-done.15.refs_14_) | copy-start | bytes 786436
  92.3 10.8 %copy-start.24 = (bf16[256,512]{1,0:T(8,128)(2,1)}, bf16[256,512]{1,0:T(8,128)(2,1)S(1)}, u32[]{:S(2)}) copy-start(bf16[256,512]{1,0:T(8,128)(2,1)S(1)} %collective-permute-done.16.refs_15_) | copy-start | bytes 786436
  92.3 10.8 %copy-start.25 = (bf16[256,512]{1,0:T(8,128)(2,1)}, bf16[256,512]{1,0:T(8,128)(2,1)S(1)}, u32[]{:S(2)}) copy-start(bf16[256,512]{1,0:T(8,128)(2,1)S(1)} %collective-permute-done.17.refs_16_) | copy-start | bytes 786436
  103.1 18.8 %all-to-all-start.4 = ((bf16[32,8,1024]{2,1,0:T(8,128)(2,1)}), bf16[32,8,1024]{2,1,0:T(8,128)(2,1)S(1)}, u32[]{:S(2)}, u32[]{:S(2)}) async-start(bf16[32,8,1024]{2,1,0:T(8,128)(2,1)} %get-tuple-element.88), calls=%async_computation.4 | async-start | bytes 1048576 | tf_op jit(solution)/shard_map/all_to_all | solution.py:511
  128.6 20.3 %all-to-all-start.5 = ((f32[64,4,128]{2,1,0:T(4,128)}), f32[64,4,128]{2,1,0:T(4,128)S(1)}, u32[]{:S(2)}, u32[]{:S(2)}) async-start(f32[64,4,128]{2,1,0:T(4,128)} %get-tuple-element.91), calls=%async_computation.5 | async-start | bytes 262144 | tf_op jit(solution)/shard_map/all_to_all | solution.py:511
  137.8 11.1 %copy-start.3 = (bf16[8,8,1152]{2,1,0:T(8,128)(2,1)S(1)}, bf16[8,8,1152]{2,1,0:T(8,128)(2,1)}, u32[]{:S(2)}) copy-start(bf16[8,8,1152]{2,1,0:T(8,128)(2,1)} %copy-done.2) | copy-start | bytes 442372
  137.8 11.1 %copy-start.5 = (f32[8,1024]{1,0:T(8,128)S(1)}, f32[8,1024]{1,0:T(8,128)}, u32[]{:S(2)}) copy-start(f32[8,1024]{1,0:T(8,128)} %copy-done.4) | copy-start | bytes 98308
  137.8 11.1 %copy-start.6 = (s32[11]{0:T(128)S(1)}, s32[11]{0:T(128)}, u32[]{:S(2)}) copy-start(s32[11]{0:T(128)} %pad_add_fusion.refs_0_.pos) | copy-start | bytes 136
  137.8 11.1 %copy-start.7 = (f32[1024,256]{1,0:T(8,128)S(1)}, f32[1024,256]{1,0:T(8,128)}, u32[]{:S(2)}) copy-start(f32[1024,256]{1,0:T(8,128)} %get-tuple-element.96.student_part) | copy-start | bytes 3145732
  137.8 11.1 %copy-start.8 = (bf16[1024,256]{1,0:T(8,128)(2,1)S(1)}, bf16[1024,256]{1,0:T(8,128)(2,1)}, u32[]{:S(2)}) copy-start(bf16[1024,256]{1,0:T(8,128)(2,1)} %get-tuple-element.85.dirs) | copy-start | bytes 1572868
  137.8 11.1 %copy-start.9 = (f32[512,256]{1,0:T(8,128)S(1)}, f32[512,256]{1,0:T(8,128)}, u32[]{:S(2)}) copy-start(f32[512,256]{1,0:T(8,128)} %get-tuple-element.97.s_mix) | copy-start | bytes 1572868
  157.9 1.7 collective-permute-start.18
  159.8 5.3 %collective-permute-start.21 = (bf16[272,256]{1,0:T(8,128)(2,1)S(1)}, bf16[272,256]{1,0:T(8,128)(2,1)S(1)}, u32[]{:S(2)}, u32[]{:S(2)}) collective-permute-start(bf16[272,256]{1,0:T(8,128)(2,1)S(1)} %get-tuple-element.118), channel_id=1, source_target_pairs={{0,6},{2,0},{4,2},{6,4},{1,7},{3,1},{5,3},{7,5},{8,14},{10,8},{12,... | collective-permute-start | bytes 417800 | tf_op jit(solution)/shard_map/ppermute | solution.py:520
  160.5 6.4 %collective-permute-start.20 = (bf16[272,256]{1,0:T(8,128)(2,1)S(1)}, bf16[272,256]{1,0:T(8,128)(2,1)S(1)}, u32[]{:S(2)}, u32[]{:S(2)}) collective-permute-start(bf16[272,256]{1,0:T(8,128)(2,1)S(1)} %get-tuple-element.118), channel_id=1, source_target_pairs={{0,2},{2,4},{4,6},{6,0},{1,3},{3,5},{5,7},{7,1},{8,10},{10,12},{12... | collective-permute-start | bytes 417800 | tf_op jit(solution)/shard_map/ppermute | solution.py:520
  161.4 7.3 %collective-permute-start.19 = (bf16[272,256]{1,0:T(8,128)(2,1)S(1)}, bf16[272,256]{1,0:T(8,128)(2,1)S(1)}, u32[]{:S(2)}, u32[]{:S(2)}) collective-permute-start(bf16[272,256]{1,0:T(8,128)(2,1)S(1)} %get-tuple-element.118), channel_id=1, source_target_pairs={{0,4},{2,6},{4,0},{6,2},{1,5},{3,7},{5,1},{7,3},{8,12},{10,14},{12... | collective-permute-start | bytes 417800 | tf_op jit(solution)/shard_map/ppermute | solution.py:520
  162.6 8.6 %collective-permute-start.25 = (bf16[256,256]{1,0:T(8,128)(2,1)S(1)}, bf16[256,256]{1,0:T(8,128)(2,1)S(1)}, u32[]{:S(2)}, u32[]{:S(2)}) collective-permute-start(bf16[256,256]{1,0:T(8,128)(2,1)S(1)} %get-tuple-element.106), channel_id=1, source_target_pairs={{0,192},{64,0},{128,64},{192,128},{1,193},{65,1},{129,65},{193,129... | collective-permute-start | bytes 393224 | tf_op jit(solution)/shard_map/ppermute | solution.py:520
  164.6 6.5 %collective-permute-start.24 = (bf16[256,256]{1,0:T(8,128)(2,1)S(1)}, bf16[256,256]{1,0:T(8,128)(2,1)S(1)}, u32[]{:S(2)}, u32[]{:S(2)}) collective-permute-start(bf16[256,256]{1,0:T(8,128)(2,1)S(1)} %get-tuple-element.105), channel_id=1, source_target_pairs={{0,128},{64,192},{128,0},{192,64},{1,129},{65,193},{129,1},{193,65... | collective-permute-start | bytes 393224 | tf_op jit(solution)/shard_map/ppermute | solution.py:520
  165.1 8.4 %collective-permute-start.23 = (bf16[256,256]{1,0:T(8,128)(2,1)S(1)}, bf16[256,256]{1,0:T(8,128)(2,1)S(1)}, u32[]{:S(2)}, u32[]{:S(2)}) collective-permute-start(bf16[256,256]{1,0:T(8,128)(2,1)S(1)} %get-tuple-element.104), channel_id=1, source_target_pairs={{0,64},{64,128},{128,192},{192,0},{1,65},{65,129},{129,193},{193,1... | collective-permute-start | bytes 393224 | tf_op jit(solution)/shard_map/ppermute | solution.py:520
  168.9 5.4 %collective-permute-start.22 = (bf16[272,256]{1,0:T(8,128)(2,1)S(1)}, bf16[272,256]{1,0:T(8,128)(2,1)S(1)}, u32[]{:S(2)}, u32[]{:S(2)}) collective-permute-start(bf16[272,256]{1,0:T(8,128)(2,1)S(1)} %maximum_maximum_fusion.1), channel_id=1, source_target_pairs={{0,1},{1,0},{2,3},{3,2},{4,5},{5,4},{6,7},{7,6},{8,9},{9,8},{10,11... | collective-permute-start | bytes 417800 | tf_op jit(solution)/shard_map/ppermute | solution.py:515
  (8 other events, 52.0 us)

commit v2 on v1

--- a/solution.py
+++ b/solution.py
@@ -340,7 +340,7 @@
         2 * ROWS * COLS * DIM,
         ROWS * COLS * 2 + COLS * DIM * 2,
         "mix_pass",
-    )(expo, col, dirs, feat)
+    )(expo, pltpu.with_memory_space_constraint(col, pltpu.VMEM), dirs, feat)
 
 
 def early_kernel(*refs):
@@ -360,7 +360,7 @@
         copy.wait()
     dirs_o[...] = unit_rows(t_s[...])
 
-    @pl.loop(0, NZ)
+    @pl.loop(0, NZ, unroll=2)
     def _(k):
         pltpu.make_async_copy(mine[0], raw_s.at[k, core], sems.at[0, k]).wait()
         pltpu.make_async_copy(other[0], raw_s.at[k, 1 - core], sems.at[1, k]).wait()

time: 176 us -> 175 us (level)
    unnamed x54 -> x50, local copies, waits for them, and re-layouts: 7.48 us -> 6.86 us
  transfers between devices with their start and end apart: 29 -> 29, of which waited for: 9 -> 10; matrix products, arithmetic and copies ran while one was open for 1% -> 1% of each run, Pallas kernels for 26% -> 25%
where the time goes in v2:
time: 175 us; the launch traced here: 174 us
  Pallas kernels  59.8 us (34%)
  starting transfers between devices  54.9 us (31%)
  blocking collectives  30.6 us (17%)
  waiting for transfers between devices  16.6 us (9%)
  local copies, waits for them, and re-layouts  7.97 us (5%)
  other arithmetic  3.27 us (2%)
    all_to_all x3, blocking collectives, gather(): return lax.all_to_all(a, axes, 0, 0)  30.6 us
    all_to_all x3, starting transfers between devices, gather(): return lax.all_to_all(a, axes, 0, 0)  21.9 us
    ppermute x16, starting transfers between devices, shift(): return lax.ppermute(a, axis, [(i, (i + by) % n) for i in range(n)])  21.6 us
    pallas_call x1, Pallas kernels, early(): call(early_kernel, [SCALARS] + [ANY] * (2 * NZ + 3), [ANY, INSIDE, INSIDE...  12.7 us
    ppermute x10, starting transfers between devices, swap_core(): return lax.ppermute(a, 'c', [(0, 1), (1, 0)])  11.4 us
    ppermute x16, waiting for transfers between devices, shift(): return lax.ppermute(a, axis, [(i, (i + by) % n) for i in range(n)])  11.3 us
    pallas_call x1, Pallas kernels, student(): call(student_kernel, [ANY, ANY], [ANY, INSIDE, INSIDE], [shape((NB, BK, D...  10.7 us
    pallas_call x1, Pallas kernels, proto_part(): call(grad_kernel, [SCALARS, ANY, ANY, INSIDE, ANY, ANY, INSIDE, ANY, OUTS...  8.98 us
  transfers between devices with their start and end apart: 29, of which 10 were waited for; matrix products, arithmetic and copies ran while one was open for 1% of the time, Pallas kernels for 25%

profile of v2, /device:TPU:1, one launch (start us, length us, event | category | flops | bytes accessed | tf_op | source)
XLA Modules:
  0.0 174.4 jit_solution(16709452810058065482)
XLA Ops:
  0.6 1.0 constant_dynamic-slice_fusion
  1.7 2.5 %collective-permute-start = (bf16[256,512]{1,0:T(8,128)(2,1)S(1)}, bf16[256,512]{1,0:T(8,128)(2,1)S(1)}, u32[]{:S(2)}, u32[]{:S(2)}) collective-permute-start(bf16[256,512]{1,0:T(8,128)(2,1)S(1)} %pad_maximum_fusion.refs_1_), channel_id=1, source_target_pairs={{0,8},{8,16},{16,24},{24,32},{32,40},{40,48},{48,56},{56,0},{1,9},... | collective-permute-start | bytes 786440 | tf_op jit(solution)/shard_map/ppermute | solution.py:520
  4.2 4.0 %collective-permute-start.1 = (bf16[256,512]{1,0:T(8,128)(2,1)S(1)}, bf16[256,512]{1,0:T(8,128)(2,1)S(1)}, u32[]{:S(2)}, u32[]{:S(2)}) collective-permute-start(bf16[256,512]{1,0:T(8,128)(2,1)S(1)} %pad_maximum_fusion.refs_1_), channel_id=1, source_target_pairs={{0,56},{8,0},{16,8},{24,16},{32,24},{40,32},{48,40},{56,48},{1,57}... | collective-permute-start | bytes 786440 | tf_op jit(solution)/shard_map/ppermute | solution.py:520
  8.2 8.9 %teacher.1 = (bf16[8,512,1024]{2,1,0:T(8,128)(2,1)}, bf16[32,8,1024]{2,1,0:T(8,128)(2,1)}) custom-call(bf16[512,256]{1,0:T(8,128)(2,1)} %feat.3, bf16[8,1024,256]{2,1,0:T(8,128)(2,1)} %bitcast.18), custom_call_target="tpu_custom_call" | custom-call | flops 2147483648 | bytes 12582912 | tf_op jit(solution)/shard_map/teacher/pallas_call | solution.py:127
  17.2 8.1 %all-to-all-start = ((bf16[32,8,1024]{2,1,0:T(8,128)(2,1)}), bf16[32,8,1024]{2,1,0:T(8,128)(2,1)S(1)}, u32[]{:S(2)}, u32[]{:S(2)}) async-start(bf16[32,8,1024]{2,1,0:T(8,128)(2,1)} %get-tuple-element.58), calls=%async_computation | async-start | bytes 1048576 | tf_op jit(solution)/shard_map/all_to_all | solution.py:511
  25.3 1.6 collective-permute-start.4
  26.9 1.5 collective-permute-start.2
  28.8 1.2 collective-permute-start.3
  30.4 10.7 %student.1 = (bf16[8,1024,256]{2,1,0:T(8,128)(2,1)}, f32[4,128]{1,0:T(4,128)}, f32[512,256]{1,0:T(8,128)}) custom-call(bf16[512,256]{1,0:T(8,128)(2,1)} %feat.5, bf16[8,1024,256]{2,1,0:T(8,128)(2,1)} %bitcast.17), custom_call_target="tpu_custom_call" | custom-call | flops 4294967296 | bytes 8388608 | tf_op jit(solution)/shard_map/student/pallas_call | solution.py:179
  41.1 3.5 %collective-permute-done.2.refs_4_ = bf16[256,512]{1,0:T(8,128)(2,1)S(1)} collective-permute-done((bf16[256,512]{1,0:T(8,128)(2,1)S(1)}, bf16[256,512]{1,0:T(8,128)(2,1)S(1)}, u32[]{:S(2)}, u32[]{:S(2)}) %collective-permute-start.2) | collective-permute-done | bytes 262176 | tf_op jit(solution)/shard_map/ppermute | solution.py:520
  44.9 2.5 %collective-permute-start.8 = (bf16[256,512]{1,0:T(8,128)(2,1)S(1)}, bf16[256,512]{1,0:T(8,128)(2,1)S(1)}, u32[]{:S(2)}, u32[]{:S(2)}) collective-permute-start(bf16[256,512]{1,0:T(8,128)(2,1)S(1)} %collective-permute-done.3.refs_5_), channel_id=1, source_target_pairs={{0,56},{8,0},{16,8},{24,16},{32,24},{40,32},{48,40},{56,48},{1,57}... | collective-permute-start | bytes 786440 | tf_op jit(solution)/shard_map/ppermute | solution.py:520
  47.4 2.3 %collective-permute-start.9 = (bf16[256,512]{1,0:T(8,128)(2,1)S(1)}, bf16[256,512]{1,0:T(8,128)(2,1)S(1)}, u32[]{:S(2)}, u32[]{:S(2)}) collective-permute-start(bf16[256,512]{1,0:T(8,128)(2,1)S(1)} %collective-permute-done.2.refs_4_), channel_id=1, source_target_pairs={{0,1},{1,0},{2,3},{3,2},{4,5},{5,4},{6,7},{7,6},{8,9},{9,8},{10,11... | collective-permute-start | bytes 786440 | tf_op jit(solution)/shard_map/ppermute | solution.py:515
  49.7 3.4 %copy-done = bf16[8,512,1024]{2,1,0:T(8,128)(2,1)S(1)} copy-done((bf16[8,512,1024]{2,1,0:T(8,128)(2,1)S(1)}, bf16[8,512,1024]{2,1,0:T(8,128)(2,1)}, u32[]{:S(2)}) %copy-start) | copy-done | bytes 8388632
  53.1 1.9 %row_pass.2 = f32[8,8,128]{2,1,0:T(8,128)S(1)} custom-call(bf16[8,512,1024]{2,1,0:T(8,128)(2,1)S(1)} %copy-done, bf16[32,8,1024]{2,1,0:T(8,128)(2,1)S(1)} %all-to-all-done.got, f32[4,128]{1,0:T(4,128)} %get-tuple-element.64.tot), custom_call_target="tpu_custom_call" | custom-call | flops 8388608 | bytes 65536 | tf_op jit(solution)/shard_map/row_pass/pallas_call | solution.py:235
  55.2 10.2 %all_to_all.30.got = f32[8,8,128]{2,1,0:T(8,128)S(1)} all-to-all(f32[8,8,128]{2,1,0:T(8,128)S(1)} %row_pass.2), channel_id=1, replica_groups=mesh['x'=4,'z'=8,'y'=4,'c'=2] {'y','c'}, dimensions={0} | all-to-all | bytes 65536 | tf_op jit(solution)/shard_map/all_to_all | solution.py:511
  65.5 1.9 %col_pass.2 = (bf16[1,8,1024]{2,1,0:T(8,128)(2,1)S(1)}, bf16[8,128]{1,0:T(8,128)(2,1)S(1)}) custom-call(bf16[8,512,1024]{2,1,0:T(8,128)(2,1)S(1)} %copy-done, f32[8,8,128]{2,1,0:T(8,128)S(1)} %all_to_all.30.got), custom_call_target="tpu_custom_call" | custom-call | flops 8388608 | bytes 1048576 | tf_op jit(solution)/shard_map/col_pass/pallas_call | solution.py:289
  67.4 2.5 %collective-permute-start.14 = (bf16[8,1024]{1,0:T(8,128)(2,1)S(1)}, bf16[8,1024]{1,0:T(8,128)(2,1)S(1)}, u32[]{:S(2)}, u32[]{:S(2)}) collective-permute-start(bf16[8,1024]{1,0:T(8,128)(2,1)S(1)} %bitcast.12), channel_id=1, source_target_pairs={{0,192},{64,0},{128,64},{192,128},{1,193},{65,1},{129,65},{193,129... | collective-permute-start | bytes 49160 | tf_op jit(solution)/shard_map/ppermute | solution.py:520
  69.9 1.7 collective-permute-start.12
  71.6 2.1 %collective-permute-done.13 = bf16[8,1024]{1,0:T(8,128)(2,1)S(1)} collective-permute-done((bf16[8,1024]{1,0:T(8,128)(2,1)S(1)}, bf16[8,1024]{1,0:T(8,128)(2,1)S(1)}, u32[]{:S(2)}, u32[]{:S(2)}) %collective-permute-start.13) | collective-permute-done | bytes 16416 | tf_op jit(solution)/shard_map/ppermute | solution.py:520
  74.0 12.3 %all_to_all.31.got.refs_19_ = bf16[8,8,1152]{2,1,0:T(8,128)(2,1)S(1)} all-to-all(bf16[8,8,1152]{2,1,0:T(8,128)(2,1)S(1)} %broadcast_in_dim.2), channel_id=1, replica_groups=mesh['x'=4,'z'=8,'y'=4,'c'=2] {'z'}, dimensions={0} | all-to-all | bytes 294912 | tf_op jit(solution)/shard_map/all_to_all | solution.py:511
  86.4 3.5 %collective-permute-start.15 = (bf16[256,512]{1,0:T(8,128)(2,1)S(1)}, bf16[256,512]{1,0:T(8,128)(2,1)S(1)}, u32[]{:S(2)}, u32[]{:S(2)}) collective-permute-start(bf16[256,512]{1,0:T(8,128)(2,1)S(1)} %collective-permute-done.7.refs_6_), channel_id=1, source_target_pairs={{0,1},{1,0},{2,3},{3,2},{4,5},{5,4},{6,7},{7,6},{8,9},{9,8},{10,11... | collective-permute-start | bytes 786440 | tf_op jit(solution)/shard_map/ppermute | solution.py:515
  90.4 1.9 %row_pass.3 = f32[8,8,128]{2,1,0:T(8,128)S(1)} custom-call(bf16[8,512,1024]{2,1,0:T(8,128)(2,1)S(1)} %copy-done, bf16[8,8,1152]{2,1,0:T(8,128)(2,1)S(1)} %all_to_all.31.got.refs_19_, f32[4,128]{1,0:T(4,128)} %get-tuple-element.64.tot), custom_call_target="tpu_custom_call" | custom-call | flops 8388608 | bytes 65536 | tf_op jit(solution)/shard_map/row_pass/pallas_call | solution.py:235
  92.3 8.0 %all_to_all.32.got = f32[8,8,128]{2,1,0:T(8,128)S(1)} all-to-all(f32[8,8,128]{2,1,0:T(8,128)S(1)} %row_pass.3), channel_id=1, replica_groups=mesh['x'=4,'z'=8,'y'=4,'c'=2] {'y','c'}, dimensions={0} | all-to-all | bytes 65536 | tf_op jit(solution)/shard_map/all_to_all | solution.py:511
  100.4 2.8 %col_pass.3 = (bf16[32,8,1024]{2,1,0:T(8,128)(2,1)}, bf16[8,128]{1,0:T(8,128)(2,1)}) custom-call(bf16[8,512,1024]{2,1,0:T(8,128)(2,1)S(1)} %copy-done, f32[8,8,128]{2,1,0:T(8,128)S(1)} %all_to_all.32.got), custom_call_target="tpu_custom_call" | custom-call | flops 8388608 | bytes 1048576 | tf_op jit(solution)/shard_map/col_pass/pallas_call | solution.py:289
  103.1 4.6 %all-to-all-start.4 = ((bf16[32,8,1024]{2,1,0:T(8,128)(2,1)}), bf16[32,8,1024]{2,1,0:T(8,128)(2,1)S(1)}, u32[]{:S(2)}, u32[]{:S(2)}) async-start(bf16[32,8,1024]{2,1,0:T(8,128)(2,1)} %get-tuple-element.88), calls=%async_computation.4 | async-start | bytes 1048576 | tf_op jit(solution)/shard_map/all_to_all | solution.py:511
  107.8 0.6 pad_add_fusion.refs_0_.pos
  108.4 12.7 %early.1 = (bf16[8,512,512]{2,1,0:T(8,128)(2,1)}, bf16[1024,256]{1,0:T(8,128)(2,1)}, f32[1024,256]{1,0:T(8,128)}) custom-call(s32[11]{0:T(128)} %pad_add_fusion.refs_0_.pos, bf16[256,512]{1,0:T(8,128)(2,1)} %copy-done.8, bf16[256,512]{1,0:T(8,128)(2,1)} %copy-done.9, bf16[256,512]{1,0:T(8,128)(2,1)} %copy-done.10, bf16[256,512]{1,0:T(8,128)(2,1)} %copy-done.12, ...), custom_call_target="tpu_custom_call" | custom-call | flops 4294967296 | bytes 4194304 | tf_op jit(solution)/shard_map/early/pallas_call | solution.py:385
  121.1 0.9 all-to-all-done.4.got
  122.0 3.4 %copy-done.1 = bf16[8,512,1024]{2,1,0:T(8,128)(2,1)S(1)} copy-done((bf16[8,512,1024]{2,1,0:T(8,128)(2,1)S(1)}, bf16[8,512,1024]{2,1,0:T(8,128)(2,1)}, u32[]{:S(2)}) %copy-start.1) | copy-done | bytes 8388632
  125.3 2.6 %row_last.1 = (f32[64,4,128]{2,1,0:T(4,128)}, f32[8,1024]{1,0:T(8,128)S(1)}) custom-call(bf16[8,512,1024]{2,1,0:T(8,128)(2,1)S(1)} %copy-done.1, bf16[32,8,1024]{2,1,0:T(8,128)(2,1)S(1)} %all-to-all-done.4.got), custom_call_target="tpu_custom_call" | custom-call | flops 8388608 | bytes 65536 | tf_op jit(solution)/shard_map/row_last/pallas_call | solution.py:254
  127.9 9.2 %all-to-all-start.5 = ((f32[64,4,128]{2,1,0:T(4,128)}), f32[64,4,128]{2,1,0:T(4,128)S(1)}, u32[]{:S(2)}, u32[]{:S(2)}) async-start(f32[64,4,128]{2,1,0:T(4,128)} %get-tuple-element.91), calls=%async_computation.5 | async-start | bytes 262144 | tf_op jit(solution)/shard_map/all_to_all | solution.py:511
  137.2 7.6 %mix_pass.1 = (f32[512,256]{1,0:T(8,128)}, f32[1,512]{1,0:T(1,128)}) custom-call(bf16[8,512,1024]{2,1,0:T(8,128)(2,1)} %get-tuple-element.62.expo, f32[8,1024]{1,0:T(8,128)S(1)} %get-tuple-element.92.col, bf16[8,1024,256]{2,1,0:T(8,128)(2,1)} %get-tuple-element.84.dirs, bf16[512,256]{1,0:T(8,128)(2,1)} %feat.5), custom_call_target="tpu_custom_call" | custom-call | flops 2147483648 | bytes 12582912 | tf_op jit(solution)/shard_map/mix_pass/pallas_call | solution.py:327
  144.8 3.5 %all-to-all-done.5 = f32[64,4,128]{2,1,0:T(4,128)S(1)} async-done(((f32[64,4,128]{2,1,0:T(4,128)}), f32[64,4,128]{2,1,0:T(4,128)S(1)}, u32[]{:S(2)}, u32[]{:S(2)}) %all-to-all-start.5) | async-done | bytes 131104 | tf_op jit(solution)/shard_map/all_to_all | solution.py:511
  148.3 9.0 %proto_part.1 = (f32[256,256]{1,0:T(8,128)S(1)}, bf16[256,256]{1,0:T(8,128)(2,1)S(1)}, bf16[256,256]{1,0:T(8,128)(2,1)S(1)}, bf16[256,256]{1,0:T(8,128)(2,1)S(1)...) custom-call(s32[11]{0:T(128)S(1)} %copy-done.4, bf16[1024,256]{1,0:T(8,128)(2,1)S(1)} %copy-done.6, ...), custom_call_target="tpu_custom_call" | custom-call | flops 4294967296 | bytes 4194304 | tf_op jit(solution)/shard_map/proto_part/pallas_call | solution.py:478
  157.3 0.5 collective-permute-start.18
  157.8 0.9 collective-permute-done.18
  159.0 0.7 collective-permute-start.21
  159.6 0.9 collective-permute-start.20
  160.5 1.2 collective-permute-start.19
  161.7 1.6 collective-permute-start.25
  163.3 0.6 collective-permute-start.24
  164.4 1.6 collective-permute-done.20
  166.0 1.8 %collective-permute-done.19 = bf16[272,256]{1,0:T(8,128)(2,1)S(1)} collective-permute-done((bf16[272,256]{1,0:T(8,128)(2,1)S(1)}, bf16[272,256]{1,0:T(8,128)(2,1)S(1)}, u32[]{:S(2)}, u32[]{:S(2)}) %collective-permute-start.19) | collective-permute-done | bytes 139296 | tf_op jit(solution)/shard_map/ppermute | solution.py:520
  168.1 2.2 %collective-permute-start.22 = (bf16[272,256]{1,0:T(8,128)(2,1)S(1)}, bf16[272,256]{1,0:T(8,128)(2,1)S(1)}, u32[]{:S(2)}, u32[]{:S(2)}) collective-permute-start(bf16[272,256]{1,0:T(8,128)(2,1)S(1)} %maximum_maximum_fusion.1), channel_id=1, source_target_pairs={{0,1},{1,0},{2,3},{3,2},{4,5},{5,4},{6,7},{7,6},{8,9},{9,8},{10,11... | collective-permute-start | bytes 417800 | tf_op jit(solution)/shard_map/ppermute | solution.py:515
  170.3 1.9 %collective-permute-done.23 = bf16[256,256]{1,0:T(8,128)(2,1)S(1)} collective-permute-done((bf16[256,256]{1,0:T(8,128)(2,1)S(1)}, bf16[256,256]{1,0:T(8,128)(2,1)S(1)}, u32[]{:S(2)}, u32[]{:S(2)}) %collective-permute-start.23) | collective-permute-done | bytes 131104 | tf_op jit(solution)/shard_map/ppermute | solution.py:520
  172.2 0.7 add_convert_fusion
  173.1 0.7 pad_maximum_fusion.1
  173.8 0.6 maximum_subtract_fusion
  (102 shorter events, 3.4 us)
Async XLA Ops:
  1.7 23.6 %copy-start.8 = (bf16[256,512]{1,0:T(8,128)(2,1)}, bf16[256,512]{1,0:T(8,128)(2,1)S(1)}, u32[]{:S(2)}) copy-start(bf16[256,512]{1,0:T(8,128)(2,1)S(1)} %pad_maximum_fusion.refs_1_) | copy-start | bytes 786436
  1.7 15.5 %collective-permute-start = (bf16[256,512]{1,0:T(8,128)(2,1)S(1)}, bf16[256,512]{1,0:T(8,128)(2,1)S(1)}, u32[]{:S(2)}, u32[]{:S(2)}) collective-permute-start(bf16[256,512]{1,0:T(8,128)(2,1)S(1)} %pad_maximum_fusion.refs_1_), channel_id=1, source_target_pairs={{0,8},{8,16},{16,24},{24,32},{32,40},{40,48},{48,56},{56,0},{1,9},... | collective-permute-start | bytes 786440 | tf_op jit(solution)/shard_map/ppermute | solution.py:520
  4.2 13.0 %collective-permute-start.1 = (bf16[256,512]{1,0:T(8,128)(2,1)S(1)}, bf16[256,512]{1,0:T(8,128)(2,1)S(1)}, u32[]{:S(2)}, u32[]{:S(2)}) collective-permute-start(bf16[256,512]{1,0:T(8,128)(2,1)S(1)} %pad_maximum_fusion.refs_1_), channel_id=1, source_target_pairs={{0,56},{8,0},{16,8},{24,16},{32,24},{40,32},{48,40},{56,48},{1,57}... | collective-permute-start | bytes 786440 | tf_op jit(solution)/shard_map/ppermute | solution.py:520
  17.2 23.9 %copy-start.9 = (bf16[256,512]{1,0:T(8,128)(2,1)}, bf16[256,512]{1,0:T(8,128)(2,1)S(1)}, u32[]{:S(2)}) copy-start(bf16[256,512]{1,0:T(8,128)(2,1)S(1)} %collective-permute-done.refs_2_) | copy-start | bytes 786436
  17.2 23.9 %copy-start.10 = (bf16[256,512]{1,0:T(8,128)(2,1)}, bf16[256,512]{1,0:T(8,128)(2,1)S(1)}, u32[]{:S(2)}) copy-start(bf16[256,512]{1,0:T(8,128)(2,1)S(1)} %collective-permute-done.1.refs_3_) | copy-start | bytes 786436
  17.2 27.4 %all-to-all-start = ((bf16[32,8,1024]{2,1,0:T(8,128)(2,1)}), bf16[32,8,1024]{2,1,0:T(8,128)(2,1)S(1)}, u32[]{:S(2)}, u32[]{:S(2)}) async-start(bf16[32,8,1024]{2,1,0:T(8,128)(2,1)} %get-tuple-element.58), calls=%async_computation | async-start | bytes 1048576 | tf_op jit(solution)/shard_map/all_to_all | solution.py:511
  25.3 15.8 %collective-permute-start.4 = (bf16[256,512]{1,0:T(8,128)(2,1)S(1)}, bf16[256,512]{1,0:T(8,128)(2,1)S(1)}, u32[]{:S(2)}, u32[]{:S(2)}) collective-permute-start(bf16[256,512]{1,0:T(8,128)(2,1)S(1)} %pad_maximum_fusion.refs_1_), channel_id=1, source_target_pairs={{0,1},{1,0},{2,3},{3,2},{4,5},{5,4},{6,7},{7,6},{8,9},{9,8},{10,11... | collective-permute-start | bytes 786440 | tf_op jit(solution)/shard_map/ppermute | solution.py:515
  26.9 17.7 %collective-permute-start.2 = (bf16[256,512]{1,0:T(8,128)(2,1)S(1)}, bf16[256,512]{1,0:T(8,128)(2,1)S(1)}, u32[]{:S(2)}, u32[]{:S(2)}) collective-permute-start(bf16[256,512]{1,0:T(8,128)(2,1)S(1)} %collective-permute-done.refs_2_), channel_id=1, source_target_pairs={{0,8},{8,16},{16,24},{24,32},{32,40},{40,48},{48,56},{56,0},{1,9},... | collective-permute-start | bytes 786440 | tf_op jit(solution)/shard_map/ppermute | solution.py:520
  28.4 16.2 %collective-permute-start.5 = (bf16[256,512]{1,0:T(8,128)(2,1)S(1)}, bf16[256,512]{1,0:T(8,128)(2,1)S(1)}, u32[]{:S(2)}, u32[]{:S(2)}) collective-permute-start(bf16[256,512]{1,0:T(8,128)(2,1)S(1)} %collective-permute-done.refs_2_), channel_id=1, source_target_pairs={{0,1},{1,0},{2,3},{3,2},{4,5},{5,4},{6,7},{7,6},{8,9},{9,8},{10,11... | collective-permute-start | bytes 786440 | tf_op jit(solution)/shard_map/ppermute | solution.py:515
  28.8 15.8 %collective-permute-start.3 = (bf16[256,512]{1,0:T(8,128)(2,1)S(1)}, bf16[256,512]{1,0:T(8,128)(2,1)S(1)}, u32[]{:S(2)}, u32[]{:S(2)}) collective-permute-start(bf16[256,512]{1,0:T(8,128)(2,1)S(1)} %collective-permute-done.1.refs_3_), channel_id=1, source_target_pairs={{0,56},{8,0},{16,8},{24,16},{32,24},{40,32},{48,40},{56,48},{1,57}... | collective-permute-start | bytes 786440 | tf_op jit(solution)/shard_map/ppermute | solution.py:520
  29.9 14.7 %collective-permute-start.6 = (bf16[256,512]{1,0:T(8,128)(2,1)S(1)}, bf16[256,512]{1,0:T(8,128)(2,1)S(1)}, u32[]{:S(2)}, u32[]{:S(2)}) collective-permute-start(bf16[256,512]{1,0:T(8,128)(2,1)S(1)} %collective-permute-done.1.refs_3_), channel_id=1, source_target_pairs={{0,1},{1,0},{2,3},{3,2},{4,5},{5,4},{6,7},{7,6},{8,9},{9,8},{10,11... | collective-permute-start | bytes 786440 | tf_op jit(solution)/shard_map/ppermute | solution.py:515
  41.1 13.9 %copy-start.11 = (bf16[256,512]{1,0:T(8,128)(2,1)}, bf16[256,512]{1,0:T(8,128)(2,1)S(1)}, u32[]{:S(2)}) copy-start(bf16[256,512]{1,0:T(8,128)(2,1)S(1)} %collective-permute-done.4.refs_9_) | copy-start | bytes 786436
  44.6 10.4 %copy-start.14 = (bf16[256,512]{1,0:T(8,128)(2,1)}, bf16[256,512]{1,0:T(8,128)(2,1)S(1)}, u32[]{:S(2)}) copy-start(bf16[256,512]{1,0:T(8,128)(2,1)S(1)} %collective-permute-done.3.refs_5_) | copy-start | bytes 786436
  44.6 10.4 %copy-start.13 = (bf16[256,512]{1,0:T(8,128)(2,1)}, bf16[256,512]{1,0:T(8,128)(2,1)S(1)}, u32[]{:S(2)}) copy-start(bf16[256,512]{1,0:T(8,128)(2,1)S(1)} %collective-permute-done.5.refs_10_) | copy-start | bytes 786436
  44.6 10.4 %collective-permute-start.7 = (bf16[256,512]{1,0:T(8,128)(2,1)S(1)}, bf16[256,512]{1,0:T(8,128)(2,1)S(1)}, u32[]{:S(2)}, u32[]{:S(2)}) collective-permute-start(bf16[256,512]{1,0:T(8,128)(2,1)S(1)} %collective-permute-done.2.refs_4_), channel_id=1, source_target_pairs={{0,8},{8,16},{16,24},{24,32},{32,40},{40,48},{48,56},{56,0},{1,9},... | collective-permute-start | bytes 786440 | tf_op jit(solution)/shard_map/ppermute | solution.py:520
  44.9 10.2 %collective-permute-start.8 = (bf16[256,512]{1,0:T(8,128)(2,1)S(1)}, bf16[256,512]{1,0:T(8,128)(2,1)S(1)}, u32[]{:S(2)}, u32[]{:S(2)}) collective-permute-start(bf16[256,512]{1,0:T(8,128)(2,1)S(1)} %collective-permute-done.3.refs_5_), channel_id=1, source_target_pairs={{0,56},{8,0},{16,8},{24,16},{32,24},{40,32},{48,40},{56,48},{1,57}... | collective-permute-start | bytes 786440 | tf_op jit(solution)/shard_map/ppermute | solution.py:520
  47.4 7.7 %collective-permute-start.9 = (bf16[256,512]{1,0:T(8,128)(2,1)S(1)}, bf16[256,512]{1,0:T(8,128)(2,1)S(1)}, u32[]{:S(2)}, u32[]{:S(2)}) collective-permute-start(bf16[256,512]{1,0:T(8,128)(2,1)S(1)} %collective-permute-done.2.refs_4_), channel_id=1, source_target_pairs={{0,1},{1,0},{2,3},{3,2},{4,5},{5,4},{6,7},{7,6},{8,9},{9,8},{10,11... | collective-permute-start | bytes 786440 | tf_op jit(solution)/shard_map/ppermute | solution.py:515
  49.7 5.4 %collective-permute-start.10 = (bf16[256,512]{1,0:T(8,128)(2,1)S(1)}, bf16[256,512]{1,0:T(8,128)(2,1)S(1)}, u32[]{:S(2)}, u32[]{:S(2)}) collective-permute-start(bf16[256,512]{1,0:T(8,128)(2,1)S(1)} %collective-permute-done.3.refs_5_), channel_id=1, source_target_pairs={{0,1},{1,0},{2,3},{3,2},{4,5},{5,4},{6,7},{7,6},{8,9},{9,8},{10,11... | collective-permute-start | bytes 786440 | tf_op jit(solution)/shard_map/ppermute | solution.py:515
  55.1 31.3 %copy-start.16 = (bf16[256,512]{1,0:T(8,128)(2,1)}, bf16[256,512]{1,0:T(8,128)(2,1)S(1)}, u32[]{:S(2)}) copy-start(bf16[256,512]{1,0:T(8,128)(2,1)S(1)} %collective-permute-done.7.refs_6_) | copy-start | bytes 786436
  55.1 34.8 %copy-start.17 = (bf16[256,512]{1,0:T(8,128)(2,1)}, bf16[256,512]{1,0:T(8,128)(2,1)S(1)}, u32[]{:S(2)}) copy-start(bf16[256,512]{1,0:T(8,128)(2,1)S(1)} %collective-permute-done.8.refs_7_) | copy-start | bytes 786436
  55.1 12.3 %copy-start.18 = (bf16[256,512]{1,0:T(8,128)(2,1)}, bf16[256,512]{1,0:T(8,128)(2,1)S(1)}, u32[]{:S(2)}) copy-start(bf16[256,512]{1,0:T(8,128)(2,1)S(1)} %collective-permute-done.9.refs_12_) | copy-start | bytes 786436
  55.1 12.2 %copy-start.19 = (bf16[256,512]{1,0:T(8,128)(2,1)}, bf16[256,512]{1,0:T(8,128)(2,1)S(1)}, u32[]{:S(2)}) copy-start(bf16[256,512]{1,0:T(8,128)(2,1)S(1)} %collective-permute-done.10.refs_13_) | copy-start | bytes 786436
  55.1 10.3 %collective-permute-start.11 = (bf16[256,512]{1,0:T(8,128)(2,1)S(1)}, bf16[256,512]{1,0:T(8,128)(2,1)S(1)}, u32[]{:S(2)}, u32[]{:S(2)}) collective-permute-start(bf16[256,512]{1,0:T(8,128)(2,1)S(1)} %collective-permute-done.7.refs_6_), channel_id=1, source_target_pairs={{0,8},{8,16},{16,24},{24,32},{32,40},{40,48},{48,56},{56,0},{1,9},... | collective-permute-start | bytes 786440 | tf_op jit(solution)/shard_map/ppermute | solution.py:520
  65.5 24.5 %copy-start.20 = (bf16[256,512]{1,0:T(8,128)(2,1)}, bf16[256,512]{1,0:T(8,128)(2,1)S(1)}, u32[]{:S(2)}) copy-start(bf16[256,512]{1,0:T(8,128)(2,1)S(1)} %collective-permute-done.11.refs_8_) | copy-start | bytes 786436
  67.4 4.2 %collective-permute-start.14 = (bf16[8,1024]{1,0:T(8,128)(2,1)S(1)}, bf16[8,1024]{1,0:T(8,128)(2,1)S(1)}, u32[]{:S(2)}, u32[]{:S(2)}) collective-permute-start(bf16[8,1024]{1,0:T(8,128)(2,1)S(1)} %bitcast.12), channel_id=1, source_target_pairs={{0,192},{64,0},{128,64},{192,128},{1,193},{65,1},{129,65},{193,129... | collective-permute-start | bytes 49160 | tf_op jit(solution)/shard_map/ppermute | solution.py:520
  69.9 3.8 %collective-permute-start.13 = (bf16[8,1024]{1,0:T(8,128)(2,1)S(1)}, bf16[8,1024]{1,0:T(8,128)(2,1)S(1)}, u32[]{:S(2)}, u32[]{:S(2)}) collective-permute-start(bf16[8,1024]{1,0:T(8,128)(2,1)S(1)} %bitcast.13), channel_id=1, source_target_pairs={{0,64},{64,128},{128,192},{192,0},{1,65},{65,129},{129,193},{193,1... | collective-permute-start | bytes 49160 | tf_op jit(solution)/shard_map/ppermute | solution.py:520
  69.9 4.1 %collective-permute-start.12 = (bf16[8,1024]{1,0:T(8,128)(2,1)S(1)}, bf16[8,1024]{1,0:T(8,128)(2,1)S(1)}, u32[]{:S(2)}, u32[]{:S(2)}) collective-permute-start(bf16[8,1024]{1,0:T(8,128)(2,1)S(1)} %bitcast.14), channel_id=1, source_target_pairs={{0,128},{64,192},{128,0},{192,64},{1,129},{65,193},{129,1},{193,65... | collective-permute-start | bytes 49160 | tf_op jit(solution)/shard_map/ppermute | solution.py:520
  86.4 5.9 %collective-permute-start.15 = (bf16[256,512]{1,0:T(8,128)(2,1)S(1)}, bf16[256,512]{1,0:T(8,128)(2,1)S(1)}, u32[]{:S(2)}, u32[]{:S(2)}) collective-permute-start(bf16[256,512]{1,0:T(8,128)(2,1)S(1)} %collective-permute-done.7.refs_6_), channel_id=1, source_target_pairs={{0,1},{1,0},{2,3},{3,2},{4,5},{5,4},{6,7},{7,6},{8,9},{9,8},{10,11... | collective-permute-start | bytes 786440 | tf_op jit(solution)/shard_map/ppermute | solution.py:515
  89.8 2.4 %collective-permute-start.16 = (bf16[256,512]{1,0:T(8,128)(2,1)S(1)}, bf16[256,512]{1,0:T(8,128)(2,1)S(1)}, u32[]{:S(2)}, u32[]{:S(2)}) collective-permute-start(bf16[256,512]{1,0:T(8,128)(2,1)S(1)} %collective-permute-done.8.refs_7_), channel_id=1, source_target_pairs={{0,1},{1,0},{2,3},{3,2},{4,5},{5,4},{6,7},{7,6},{8,9},{9,8},{10,11... | collective-permute-start | bytes 786440 | tf_op jit(solution)/shard_map/ppermute | solution.py:515
  89.9 2.3 %collective-permute-start.17 = (bf16[256,512]{1,0:T(8,128)(2,1)S(1)}, bf16[256,512]{1,0:T(8,128)(2,1)S(1)}, u32[]{:S(2)}, u32[]{:S(2)}) collective-permute-start(bf16[256,512]{1,0:T(8,128)(2,1)S(1)} %collective-permute-done.11.refs_8_), channel_id=1, source_target_pairs={{0,1},{1,0},{2,3},{3,2},{4,5},{5,4},{6,7},{7,6},{8,9},{9,8},{10,11... | collective-permute-start | bytes 786440 | tf_op jit(solution)/shard_map/ppermute | solution.py:515
  92.3 10.9 %copy-start.21 = (bf16[256,512]{1,0:T(8,128)(2,1)}, bf16[256,512]{1,0:T(8,128)(2,1)S(1)}, u32[]{:S(2)}) copy-start(bf16[256,512]{1,0:T(8,128)(2,1)S(1)} %collective-permute-done.15.refs_14_) | copy-start | bytes 786436
  92.3 10.8 %copy-start.22 = (bf16[256,512]{1,0:T(8,128)(2,1)}, bf16[256,512]{1,0:T(8,128)(2,1)S(1)}, u32[]{:S(2)}) copy-start(bf16[256,512]{1,0:T(8,128)(2,1)S(1)} %collective-permute-done.16.refs_15_) | copy-start | bytes 786436
  92.3 10.8 %copy-start.23 = (bf16[256,512]{1,0:T(8,128)(2,1)}, bf16[256,512]{1,0:T(8,128)(2,1)S(1)}, u32[]{:S(2)}) copy-start(bf16[256,512]{1,0:T(8,128)(2,1)S(1)} %collective-permute-done.17.refs_16_) | copy-start | bytes 786436
  103.1 18.8 %all-to-all-start.4 = ((bf16[32,8,1024]{2,1,0:T(8,128)(2,1)}), bf16[32,8,1024]{2,1,0:T(8,128)(2,1)S(1)}, u32[]{:S(2)}, u32[]{:S(2)}) async-start(bf16[32,8,1024]{2,1,0:T(8,128)(2,1)} %get-tuple-element.88), calls=%async_computation.4 | async-start | bytes 1048576 | tf_op jit(solution)/shard_map/all_to_all | solution.py:511
  127.9 20.3 %all-to-all-start.5 = ((f32[64,4,128]{2,1,0:T(4,128)}), f32[64,4,128]{2,1,0:T(4,128)S(1)}, u32[]{:S(2)}, u32[]{:S(2)}) async-start(f32[64,4,128]{2,1,0:T(4,128)} %get-tuple-element.91), calls=%async_computation.5 | async-start | bytes 262144 | tf_op jit(solution)/shard_map/all_to_all | solution.py:511
  137.1 11.1 %copy-start.3 = (bf16[8,8,1152]{2,1,0:T(8,128)(2,1)S(1)}, bf16[8,8,1152]{2,1,0:T(8,128)(2,1)}, u32[]{:S(2)}) copy-start(bf16[8,8,1152]{2,1,0:T(8,128)(2,1)} %copy-done.2) | copy-start | bytes 442372
  137.2 11.1 %copy-start.4 = (s32[11]{0:T(128)S(1)}, s32[11]{0:T(128)}, u32[]{:S(2)}) copy-start(s32[11]{0:T(128)} %pad_add_fusion.refs_0_.pos) | copy-start | bytes 136
  137.2 11.1 %copy-start.5 = (f32[1024,256]{1,0:T(8,128)S(1)}, f32[1024,256]{1,0:T(8,128)}, u32[]{:S(2)}) copy-start(f32[1024,256]{1,0:T(8,128)} %get-tuple-element.96.student_part) | copy-start | bytes 3145732
  137.2 11.1 %copy-start.6 = (bf16[1024,256]{1,0:T(8,128)(2,1)S(1)}, bf16[1024,256]{1,0:T(8,128)(2,1)}, u32[]{:S(2)}) copy-start(bf16[1024,256]{1,0:T(8,128)(2,1)} %get-tuple-element.85.dirs) | copy-start | bytes 1572868
  137.2 11.1 %copy-start.7 = (f32[512,256]{1,0:T(8,128)S(1)}, f32[512,256]{1,0:T(8,128)}, u32[]{:S(2)}) copy-start(f32[512,256]{1,0:T(8,128)} %get-tuple-element.97.s_mix) | copy-start | bytes 1572868
  157.3 1.5 collective-permute-start.18
  159.0 5.0 %collective-permute-start.21 = (bf16[272,256]{1,0:T(8,128)(2,1)S(1)}, bf16[272,256]{1,0:T(8,128)(2,1)S(1)}, u32[]{:S(2)}, u32[]{:S(2)}) collective-permute-start(bf16[272,256]{1,0:T(8,128)(2,1)S(1)} %get-tuple-element.118), channel_id=1, source_target_pairs={{0,6},{2,0},{4,2},{6,4},{1,7},{3,1},{5,3},{7,5},{8,14},{10,8},{12,... | collective-permute-start | bytes 417800 | tf_op jit(solution)/shard_map/ppermute | solution.py:520
  159.6 6.4 %collective-permute-start.20 = (bf16[272,256]{1,0:T(8,128)(2,1)S(1)}, bf16[272,256]{1,0:T(8,128)(2,1)S(1)}, u32[]{:S(2)}, u32[]{:S(2)}) collective-permute-start(bf16[272,256]{1,0:T(8,128)(2,1)S(1)} %get-tuple-element.118), channel_id=1, source_target_pairs={{0,2},{2,4},{4,6},{6,0},{1,3},{3,5},{5,7},{7,1},{8,10},{10,12},{12... | collective-permute-start | bytes 417800 | tf_op jit(solution)/shard_map/ppermute | solution.py:520
  160.5 7.3 %collective-permute-start.19 = (bf16[272,256]{1,0:T(8,128)(2,1)S(1)}, bf16[272,256]{1,0:T(8,128)(2,1)S(1)}, u32[]{:S(2)}, u32[]{:S(2)}) collective-permute-start(bf16[272,256]{1,0:T(8,128)(2,1)S(1)} %get-tuple-element.118), channel_id=1, source_target_pairs={{0,4},{2,6},{4,0},{6,2},{1,5},{3,7},{5,1},{7,3},{8,12},{10,14},{12... | collective-permute-start | bytes 417800 | tf_op jit(solution)/shard_map/ppermute | solution.py:520
  161.7 8.6 %collective-permute-start.25 = (bf16[256,256]{1,0:T(8,128)(2,1)S(1)}, bf16[256,256]{1,0:T(8,128)(2,1)S(1)}, u32[]{:S(2)}, u32[]{:S(2)}) collective-permute-start(bf16[256,256]{1,0:T(8,128)(2,1)S(1)} %get-tuple-element.106), channel_id=1, source_target_pairs={{0,192},{64,0},{128,64},{192,128},{1,193},{65,1},{129,65},{193,129... | collective-permute-start | bytes 393224 | tf_op jit(solution)/shard_map/ppermute | solution.py:520
  163.3 7.0 %collective-permute-start.24 = (bf16[256,256]{1,0:T(8,128)(2,1)S(1)}, bf16[256,256]{1,0:T(8,128)(2,1)S(1)}, u32[]{:S(2)}, u32[]{:S(2)}) collective-permute-start(bf16[256,256]{1,0:T(8,128)(2,1)S(1)} %get-tuple-element.105), channel_id=1, source_target_pairs={{0,128},{64,192},{128,0},{192,64},{1,129},{65,193},{129,1},{193,65... | collective-permute-start | bytes 393224 | tf_op jit(solution)/shard_map/ppermute | solution.py:520
  163.9 8.2 %collective-permute-start.23 = (bf16[256,256]{1,0:T(8,128)(2,1)S(1)}, bf16[256,256]{1,0:T(8,128)(2,1)S(1)}, u32[]{:S(2)}, u32[]{:S(2)}) collective-permute-start(bf16[256,256]{1,0:T(8,128)(2,1)S(1)} %get-tuple-element.104), channel_id=1, source_target_pairs={{0,64},{64,128},{128,192},{192,0},{1,65},{65,129},{129,193},{193,1... | collective-permute-start | bytes 393224 | tf_op jit(solution)/shard_map/ppermute | solution.py:520
  168.1 4.8 %collective-permute-start.22 = (bf16[272,256]{1,0:T(8,128)(2,1)S(1)}, bf16[272,256]{1,0:T(8,128)(2,1)S(1)}, u32[]{:S(2)}, u32[]{:S(2)}) collective-permute-start(bf16[272,256]{1,0:T(8,128)(2,1)S(1)} %maximum_maximum_fusion.1), channel_id=1, source_target_pairs={{0,1},{1,0},{2,3},{3,2},{4,5},{5,4},{6,7},{7,6},{8,9},{9,8},{10,11... | collective-permute-start | bytes 417800 | tf_op jit(solution)/shard_map/ppermute | solution.py:515
  (6 other events, 40.9 us)
